TPU v7x, 32 devices: a whole 2x2x4 slice. The times are simulated.
32 devices in a mesh: sens: 4 (over x, core), src: 8 (over z, y).
Axes of the slice: x: 2, y: 2, z: 4, core: 2. Of those that a mesh axis runs over, the one named last changes fastest.
Arguments:
- operator: bfloat16 [128, 2, 512, 1024], P(None, None, 'sens', 'src'), may hold values from -0.375 to 0.375
- right_side: float32 [128, 2, 32, 1024], P('sens', None, None, 'src'), may hold values from -6 to 6
- noise_weights: float32 [128, 512], P('src', 'sens'), may hold values from 0.25 to 4
- damping: float32 [128], P('sens'), may hold values from 1 to 16
Outputs:
- solution: float32 [128, 2, 32, 1024], P('sens', None, None, 'src')
- residual: float32 [128, 2, 32, 1024], P('sens', None, None, 'src')
All inputs are finite; a program needn't handle non-finite values.
Results may differ from a plain program's by a relative error of at most 0.025.
Values may be sent and summed in bfloat16 or wider, within the bound.
No kernel may reach another device: no remote copies, remote signals or barrier semaphores. Data moves between devices by JAX's collectives and lax.ppermute only.
A program may use at most 128 MiB of HBM per device.

v0:
```python
import functools

import jax
import jax.numpy as jnp
from jax import lax
from jax.experimental import pallas as pl
from jax.experimental.pallas import tpu as pltpu
from jax.sharding import PartitionSpec as P

CHUNKS = 2
KERNEL_BYTES = 16 * 2 ** 20
F32 = jnp.float32
BF16 = jnp.bfloat16
NT = (((1,), (1,)), ((), ()))
NN = (((1,), (0,)), ((), ()))


def largest_divisor(extent, most):
    return next(size for size in range(min(extent, most), 0, -1) if extent % size == 0)


def turned(block, sign):
    half = block.shape[0] // 2
    upper, lower = block[:half], block[half:]
    return jnp.concatenate([-lower, upper] if sign < 0 else [lower, -upper], axis=0)


def forward_rows(vector, near, far):
    left = jnp.concatenate([vector, turned(vector, -1)], axis=1)
    right = jnp.concatenate(
        [jnp.concatenate([part[0], part[1]], axis=1) for part in (near, far)], axis=0
    )
    return lax.dot_general(left, right, NT, preferred_element_type=F32)


def adjoint_rows(field, near, far):
    sensors = near.shape[1]
    total = None
    for part, piece in ((near, field[:, :sensors]), (far, field[:, sensors:])):
        left = jnp.concatenate([piece, turned(piece, 1)], axis=1)
        right = part.reshape(2 * sensors, part.shape[2])
        term = lax.dot_general(left, right, NN, preferred_element_type=F32)
        total = term if total is None else total + term
    return total


def cost(flops, moved):
    return pl.CostEstimate(flops=flops, bytes_accessed=moved, transcendentals=0)


class Plan:
    def __init__(self, operator, right_side, n_sens, n_src, chunks):
        self.freqs, _, self.sensors, self.sources = operator.shape
        self.block = right_side.shape[0]
        self.rows = right_side.shape[1] * right_side.shape[2]
        self.pairs = n_sens // 2
        self.groups = n_src // 2
        self.chunks = chunks
        self.part = self.block // chunks
        self.step = largest_divisor(self.part, 8)
        self.steps = self.part // self.step
        self.flops = 16 * self.part * self.rows * self.sensors * self.sources * 2
        self.piece = self.part * self.rows // self.groups


def part_spec(plan, blk_of):
    return pl.BlockSpec(
        (None, plan.step, 2, plan.sensors, plan.sources),
        lambda p, t, m: (m[0] ^ blk_of(p, m), t, 0, 0, 0),
    )


def forward_call(plan, chunk, meta, near, far, first, vectors):
    blk_of = lambda p, m: 1 - (m[2] ^ p)
    step, steps = plan.step, plan.steps

    def kernel(m, near_ref, far_ref, one_ref, two_ref, send_ref, keep_ref):
        phase = pl.program_id(0)
        blk = blk_of(phase, m)

        def run(pick, out_ref):
            for f in range(step):
                out_ref[f] = forward_rows(pick(f), near_ref[f], far_ref[f]).astype(out_ref.dtype)

        def both(pick):
            @pl.when(phase == 0)
            def _():
                run(pick, send_ref)

            @pl.when(phase == 1)
            def _():
                run(pick, keep_ref)

        if first:
            def pick(f):
                own = one_ref[f].astype(BF16)
                return jnp.where(blk == 0, own, two_ref[f])

            both(pick)
        else:
            both(lambda f: (one_ref[f].astype(F32) + two_ref[f].astype(F32)).astype(BF16))

    size = (step, plan.rows, plan.sources)
    if first:
        vec_specs = [
            pl.BlockSpec(size, lambda p, t, m: (chunk * steps + t, 0, 0)),
            pl.BlockSpec(size, lambda p, t, m: (t, 0, 0)),
        ]
    else:
        vec_specs = [
            pl.BlockSpec((None,) + size, lambda p, t, m: (blk_of(p, m), t, 0, 0)),
            pl.BlockSpec((None,) + size, lambda p, t, m: (1 - blk_of(p, m), t, 0, 0)),
        ]
    out = (step, plan.rows, 2 * plan.sensors)
    shape = (plan.part, plan.rows, 2 * plan.sensors)
    return pl.pallas_call(
        kernel,
        grid_spec=pltpu.PrefetchScalarGridSpec(
            num_scalar_prefetch=1,
            grid=(2, steps),
            in_specs=[part_spec(plan, blk_of)] * 2 + vec_specs,
            out_specs=[
                pl.BlockSpec(out, lambda p, t, m: (jnp.where(p == 0, t, steps - 1), 0, 0)),
                pl.BlockSpec(out, lambda p, t, m: (jnp.where(p == 0, 0, t), 0, 0)),
            ],
        ),
        out_shape=[jax.ShapeDtypeStruct(shape, BF16), jax.ShapeDtypeStruct(shape, F32)],
        cost_estimate=cost(plan.flops, 16 * plan.part * plan.sensors * plan.sources),
        compiler_params=pltpu.CompilerParams(vmem_limit_bytes=KERNEL_BYTES),
        name="forward",
    )(meta, near, far, *vectors)


def adjoint_call(plan, meta, near, far, halves, last):
    blk_of = lambda p, m: 1 - p
    step, steps = plan.step, plan.steps

    def kernel(m, near_ref, far_ref, own_ref, got_ref, *outs):
        phase = pl.program_id(0)
        mine = blk_of(phase, m) == m[2]

        def run(out_ref):
            for f in range(step):
                field = jnp.where(mine, own_ref[f], got_ref[f])
                out_ref[f] = adjoint_rows(field, near_ref[f], far_ref[f]).astype(out_ref.dtype)

        if last:
            @pl.when(phase == 0)
            def _():
                run(outs[0])

            @pl.when(phase == 1)
            def _():
                run(outs[1])
        else:
            run(outs[0])

    size = (step, plan.rows, 2 * plan.sensors)
    out = (step, plan.rows, plan.sources)
    shape = (plan.part, plan.rows, plan.sources)
    if last:
        out_specs = [
            pl.BlockSpec(out, lambda p, t, m: (jnp.where(p == 0, t, steps - 1), 0, 0)),
            pl.BlockSpec(out, lambda p, t, m: (jnp.where(p == 0, 0, t), 0, 0)),
        ]
        out_shape = [jax.ShapeDtypeStruct(shape, BF16), jax.ShapeDtypeStruct(shape, F32)]
    else:
        out_specs = pl.BlockSpec((None,) + out, lambda p, t, m: (blk_of(p, m), t, 0, 0))
        out_shape = jax.ShapeDtypeStruct((2,) + shape, BF16)
    return pl.pallas_call(
        kernel,
        grid_spec=pltpu.PrefetchScalarGridSpec(
            num_scalar_prefetch=1,
            grid=(2, steps),
            in_specs=[
                part_spec(plan, blk_of),
                part_spec(plan, blk_of),
                pl.BlockSpec(size, lambda p, t, m: (t, 0, 0)),
                pl.BlockSpec(size, lambda p, t, m: (t, 0, 0)),
            ],
            out_specs=out_specs,
        ),
        out_shape=out_shape,
        cost_estimate=cost(plan.flops, 16 * plan.part * plan.sensors * plan.sources),
        compiler_params=pltpu.CompilerParams(vmem_limit_bytes=KERNEL_BYTES),
        name="adjoint",
    )(meta, near, far, *halves)


def split_call(plan, meta, keep, got):
    piece, groups = plan.piece, plan.groups
    width = keep.shape[-1]

    def kernel(m, keep_ref, got_ref, mine_ref, *sends):
        for d in range(groups):
            place = pl.ds(pl.multiple_of((m[3] ^ d) * piece, piece), piece)
            total = keep_ref[place] + got_ref[place].astype(F32)
            if d == 0:
                mine_ref[...] = total
            else:
                sends[d - 1][...] = total.astype(BF16)

    whole = pl.BlockSpec(memory_space=pltpu.VMEM)
    return pl.pallas_call(
        kernel,
        in_specs=[pl.BlockSpec(memory_space=pltpu.SMEM), whole, whole],
        out_specs=[whole] * groups,
        out_shape=[jax.ShapeDtypeStruct((piece, width), F32)]
        + [jax.ShapeDtypeStruct((piece, width), BF16)] * (groups - 1),
        cost_estimate=cost(groups * piece * width, groups * piece * width * 8),
        compiler_params=pltpu.CompilerParams(vmem_limit_bytes=KERNEL_BYTES),
        name="split",
    )(meta, keep.reshape(-1, width), got.reshape(-1, width))


def place_call(plan, meta, pieces):
    piece, groups = plan.piece, plan.groups
    width = pieces[0].shape[-1]

    def kernel(m, *refs):
        for d in range(groups):
            place = pl.ds(pl.multiple_of((m[3] ^ d) * piece, piece), piece)
            refs[groups][place] = refs[d][...]

    whole = pl.BlockSpec(memory_space=pltpu.VMEM)
    out = pl.pallas_call(
        kernel,
        in_specs=[pl.BlockSpec(memory_space=pltpu.SMEM)] + [whole] * groups,
        out_specs=whole,
        out_shape=jax.ShapeDtypeStruct((groups * piece, width), BF16),
        cost_estimate=cost(0, groups * piece * width * 4),
        compiler_params=pltpu.CompilerParams(vmem_limit_bytes=KERNEL_BYTES),
        name="place",
    )(meta, *pieces)
    return out.reshape(plan.part, plan.rows, width)


def body(n_sens, n_src, operator, right_side, noise_weights, damping):
    plan = Plan(operator, right_side, n_sens, n_src, CHUNKS)
    sens, src = lax.axis_index("sens"), lax.axis_index("src")
    pair, core = sens // 2, sens % 2
    half, group = src % 2, src // 2
    meta = jnp.stack([pair, core, half, group]).astype(jnp.int32)
    part, rows, block = plan.part, plan.rows, plan.block

    def to_core(array):
        return lax.ppermute(array, "sens", [(i, i ^ 1) for i in range(n_sens)])

    def to_pair(array):
        return lax.ppermute(array, "sens", [(i, i ^ 2) for i in range(n_sens)])

    def to_half(array):
        return lax.ppermute(array, "src", [(j, j ^ 1) for j in range(n_src)])

    def to_group(array, d):
        return lax.ppermute(array, "src", [(j, j ^ (2 * d)) for j in range(n_src)])

    def src_bits():
        return [2 ** bit for bit in range(n_src.bit_length() - 1)]

    def total(values):
        sums = jnp.zeros((1, 128), F32).at[0, : len(values)].set(jnp.stack(values))
        sums = sums + to_core(sums)
        for bit in src_bits():
            sums = sums + lax.ppermute(sums, "src", [(j, j ^ bit) for j in range(n_src)])
        return (sums + to_pair(sums))[0]

    def all_weights(table):
        for bit in src_bits():
            other = lax.ppermute(table, "src", [(j, j ^ bit) for j in range(n_src)])
            low = (src // bit) % 2 == 0
            table = jnp.concatenate(
                [jnp.where(low, table, other), jnp.where(low, other, table)], axis=0
            )
        return table

    whole = operator.reshape(plan.pairs, 2, block, 2, plan.sensors, plan.sources)
    start = right_side.reshape(block, rows, plan.sources)
    chunks = range(plan.chunks)

    sent_b = [start[k * part:(k + 1) * part].astype(BF16) for k in chunks]
    got_b = [to_pair(sent) for sent in sent_b]
    core, *_ = lax.optimization_barrier((core, *sent_b))

    def half_of(k, which):
        size = (plan.pairs, 1, part, 2, plan.sensors, plan.sources)
        cut = lax.dynamic_slice(whole, (0, which, k * part, 0, 0, 0), size)
        return cut.reshape(plan.pairs, part, 2, plan.sensors, plan.sources)

    near, far = [], []
    for k in chunks:
        far.append(to_core(half_of(k, 1 - core)))
        near.append(half_of(k, core))

    weights = all_weights(noise_weights)
    weights = weights.reshape(plan.pairs, 2, block, plan.sensors)
    weights_near = lax.dynamic_index_in_dim(weights, core, 1, keepdims=False)
    weights_far = to_core(lax.dynamic_index_in_dim(weights, 1 - core, 1, keepdims=False))
    weights = jnp.concatenate([weights_near, weights_far], axis=-1)
    weights = lax.dynamic_index_in_dim(weights, pair ^ half, 0, keepdims=False)
    damping_row = jnp.where(half == 0, damping, to_pair(damping))
    count = max(1, plan.piece // rows)

    def piece_of(k, table):
        place = k * part + group * plan.piece // rows
        cut = lax.dynamic_slice_in_dim(table, place, count, 0)
        return cut.reshape(count, 1, -1)

    def reduce_field(send, keep):
        mine, *sends = split_call(plan, meta, keep, to_half(send))
        for d, piece in enumerate(sends):
            mine = mine + to_group(piece, d + 1).astype(F32)
        return mine.reshape(count, plan.piece // count, -1)

    def gather_field(weighted):
        weighted = weighted.astype(BF16).reshape(plan.piece, -1)
        pieces = [weighted] + [to_group(weighted, d) for d in range(1, plan.groups)]
        own = place_call(plan, meta, pieces)
        return own, to_half(own)

    field, products = [], []
    for k in chunks:
        send, keep = forward_call(plan, k, meta, near[k], far[k], True, (start, got_b[k]))
        field.append(reduce_field(send, keep))
    scaled = [piece_of(k, weights) * field[k] for k in chunks]
    for k in chunks:
        back = adjoint_call(plan, meta, near[k], far[k], gather_field(scaled[k]), False)
        products.append((back, to_pair(back)))
    damp = damping[:, None, None]
    norm, curve = jnp.sum(start * start), jnp.sum(damp * start * start)
    for k in chunks:
        curve = curve + jnp.sum(scaled[k] * field[k])
    sums = total([norm, curve])
    norm_0, curve_0 = sums[0], sums[1]
    alpha_0 = norm_0 / curve_0

    image_0 = jnp.concatenate([mine[0].astype(F32) + got[1].astype(F32) for mine, got in products])
    image_0 = image_0 + damp * start
    residual = start - alpha_0 * image_0
    values = [
        jnp.sum(residual * residual),
        jnp.sum(damp * residual * residual),
        jnp.sum(damp * residual * start),
    ]

    square = cross = 0.0
    final = []
    for k in chunks:
        send, keep = forward_call(plan, k, meta, near[k], far[k], False, products[k])
        factor = 1.0 - alpha_0 * piece_of(k, damping_row)
        new_field = factor * field[k] - alpha_0 * reduce_field(send, keep)
        new_scaled = piece_of(k, weights) * new_field
        square = square + jnp.sum(new_scaled * new_field)
        cross = cross + jnp.sum(new_scaled * field[k])
        other, own = adjoint_call(plan, meta, near[k], far[k], gather_field(new_scaled), True)
        final.append(own + to_pair(other).astype(F32))
    sums = total(values + [square, cross])
    norm_1 = sums[0]
    beta = norm_1 / norm_0
    curve_1 = (sums[1] + sums[3]) + 2.0 * beta * (sums[2] + sums[4]) + beta * beta * curve_0
    alpha_1 = norm_1 / curve_1

    image_1 = jnp.concatenate(final) + damp * residual + beta * image_0
    solution = alpha_0 * start + alpha_1 * (residual + beta * start)
    residual = residual - alpha_1 * image_1
    return solution.reshape(right_side.shape), residual.reshape(right_side.shape)


def solution(mesh):
    in_specs = (
        P(None, None, "sens", "src"),
        P("sens", None, None, "src"),
        P("src", "sens"),
        P("sens"),
    )
    out_specs = (P("sens", None, None, "src"), P("sens", None, None, "src"))
    shard = functools.partial(body, mesh.shape["sens"], mesh.shape["src"])
    return jax.shard_map(shard, mesh=mesh, in_specs=in_specs, out_specs=out_specs, check_vma=False)
```

profile of v0, /device:TPU:0, one launch (start us, length us, event | category | flops | bytes accessed | tf_op | source)
XLA Modules:
  0.0 266.2 jit_solution(14883128336126045410)
XLA Ops:
  0.6 2.8 %multiply_reduce_fusion.1 = (f32[]{:T(128)}, f32[]{:T(128)}, bf16[32,2,32,128]{3,2,1,0:T(8,128)(2,1)S(1)}) fusion(f32[32,2,32,128]{3,2,1,0:T(8,128)} %param.9, f32[32]{0:T(128)} %param.11), kind=kLoop, calls=%fused_computation.18 | loop fusion | flops 1572862 | bytes 1573000 | tf_op jit(solution)/shard_map/reduce_sum | solution.py:330
  4.2 8.5 %dynamic-slice_bitcast_fusion.2 = (bf16[2,16,2,128,128]{4,3,2,1,0:T(8,128)(2,1)}, bf16[2,16,2,128,128]{4,3,2,1,0:T(8,128)(2,1)S(1)}, bf16[2,16,2,128,128]{4,3,2,1,0:T(8,128)(2,1)}, bf16[2,16,2,128,128]{4,3,2,1,0:T(8,128)(2,1)}) fusion(bf16[2,2,32,2,128,128]{5,4,3,2,1,0:T(8,128)(2,1)} %bitcast.109, s32[]{:T(128)S(6)} %select_n.132, s32[]{:T(128)S(6)} %select_n.131), kind=kLoop, calls=%fused_computation.2 | loop fusion | bytes 16777224 | tf_op jit(solution)/shard_map/reshape | solution.py:288
  13.2 3.0 %collective-permute-start = (f32[16,128]{1,0:T(8,128)S(1)}, f32[16,128]{1,0:T(8,128)S(1)}, u32[]{:S(2)}, u32[]{:S(2)}) collective-permute-start(f32[16,128]{1,0:T(8,128)S(1)} %copy-done.26), channel_id=1, source_target_pairs={{0,1},{1,0},{2,3},{3,2},{4,5},{5,4},{6,7},{7,6},{8,9},{9,8},{10,11... | collective-permute-start | bytes 24584 | tf_op jit(solution)/shard_map/ppermute | solution.py:270
  20.0 2.0 collective-permute-done.1
  22.0 3.7 %collective-permute-done.5.two_ref = bf16[16,64,128]{2,1,0:T(8,128)(2,1)} collective-permute-done((bf16[16,64,128]{2,1,0:T(8,128)(2,1)}, bf16[16,64,128]{2,1,0:T(8,128)(2,1)}, u32[]{:S(2)}, u32[]{:S(2)}) %collective-permute-start.5) | collective-permute-done | bytes 262176 | tf_op jit(solution)/shard_map/ppermute | solution.py:250
  27.3 5.2 %forward.4 = (bf16[16,64,256]{2,1,0:T(8,128)(2,1)}, f32[16,64,256]{2,1,0:T(8,128)S(1)}) custom-call(s32[4]{0:T(128)S(1)} %pad_add_fusion.m, bf16[2,16,2,128,128]{4,3,2,1,0:T(8,128)(2,1)S(1)} %copy-done, bf16[2,16,2,128,128]{4,3,2,1,0:T(8,128)(2,1)} %collective-permute-done.4.far_ref, f32[32,64,128]{2,1,0:T(8,128)S(1)} %bitcast.99, ...), custom_call_target="tpu_custom_call" | custom-call | flops 536870912 | bytes 4194304 | tf_op jit(solution)/shard_map/forward/pallas_call | solution.py:116
  32.6 5.0 %forward.5 = (bf16[16,64,256]{2,1,0:T(8,128)(2,1)}, f32[16,64,256]{2,1,0:T(8,128)S(1)}) custom-call(s32[4]{0:T(128)S(1)} %pad_add_fusion.m, bf16[2,16,2,128,128]{4,3,2,1,0:T(8,128)(2,1)S(1)} %get-tuple-element.102.near_ref, bf16[2,16,2,128,128]{4,3,2,1,0:T(8,128)(2,1)} %collective-permute-done.10.far_ref, f32[32,64,128]{2,1,0:T(8,128)S(1)} %bitcast.100, ...), custom_call_target="tpu_custom_call" | custom-call | flops 536870912 | bytes 4194304 | tf_op jit(solution)/shard_map/forward/pallas_call | solution.py:116
  38.5 2.0 collective-permute-start.12
  40.5 2.6 collective-permute-start.2
  43.1 2.2 collective-permute-done.2
  52.4 2.6 collective-permute-start.8
  60.3 2.6 collective-permute-start.14
  63.1 2.6 collective-permute-done.8
  67.4 2.6 collective-permute-start.23
  70.1 11.1 %collective-permute-start.22 = (bf16[256,256]{1,0:T(8,128)(2,1)S(1)}, bf16[256,256]{1,0:T(8,128)(2,1)S(1)}, u32[]{:S(2)}, u32[]{:S(2)}) collective-permute-start(bf16[256,256]{1,0:T(8,128)(2,1)S(1)} %fusion.6.refs_0_), channel_id=1, source_target_pairs={{0,4},{1,5},{2,6},{3,7},{4,0},{5,1},{6,2},{7,3},{8,12},{9,13},{10,... | collective-permute-start | bytes 393224 | tf_op jit(solution)/shard_map/ppermute | solution.py:256
  83.0 2.4 collective-permute-start.28
  85.3 4.1 %collective-permute-start.27 = (bf16[256,256]{1,0:T(8,128)(2,1)S(1)}, bf16[256,256]{1,0:T(8,128)(2,1)S(1)}, u32[]{:S(2)}, u32[]{:S(2)}) collective-permute-start(bf16[256,256]{1,0:T(8,128)(2,1)S(1)} %fusion.8.refs_0_), channel_id=1, source_target_pairs={{0,4},{1,5},{2,6},{3,7},{4,0},{5,1},{6,2},{7,3},{8,12},{9,13},{10,... | collective-permute-start | bytes 393224 | tf_op jit(solution)/shard_map/ppermute | solution.py:256
  91.1 4.4 %collective-permute-done.22.refs_2_ = bf16[256,256]{1,0:T(8,128)(2,1)S(1)} collective-permute-done((bf16[256,256]{1,0:T(8,128)(2,1)S(1)}, bf16[256,256]{1,0:T(8,128)(2,1)S(1)}, u32[]{:S(2)}, u32[]{:S(2)}) %collective-permute-start.22) | collective-permute-done | bytes 131104 | tf_op jit(solution)/shard_map/ppermute | solution.py:256
  96.6 3.1 %collective-permute-done.27.refs_2_ = bf16[256,256]{1,0:T(8,128)(2,1)S(1)} collective-permute-done((bf16[256,256]{1,0:T(8,128)(2,1)S(1)}, bf16[256,256]{1,0:T(8,128)(2,1)S(1)}, u32[]{:S(2)}, u32[]{:S(2)}) %collective-permute-start.27) | collective-permute-done | bytes 131104 | tf_op jit(solution)/shard_map/ppermute | solution.py:256
  100.9 7.9 %collective-permute-done.24.got_ref = bf16[16,64,256]{2,1,0:T(8,128)(2,1)S(1)} collective-permute-done((bf16[16,64,256]{2,1,0:T(8,128)(2,1)S(1)}, bf16[16,64,256]{2,1,0:T(8,128)(2,1)S(1)}, u32[]{:S(2)}, u32[]{:S(2)}) %collective-permute-start.24) | collective-permute-done | bytes 524320 | tf_op jit(solution)/shard_map/ppermute | solution.py:253
  108.8 4.6 %adjoint.4.one_ref = bf16[2,16,64,128]{3,2,1,0:T(8,128)(2,1)} custom-call(s32[4]{0:T(128)S(1)} %pad_add_fusion.m, bf16[2,16,2,128,128]{4,3,2,1,0:T(8,128)(2,1)S(1)} %copy-done.1, bf16[2,16,2,128,128]{4,3,2,1,0:T(8,128)(2,1)} %collective-permute-done.4.far_ref, bf16[16,64,256]{2,1,0:T(8,128)(2,1)S(1)} %bitcast.102, ...), custom_call_target="tpu_custom_call" | custom-call | flops 536870912 | bytes 4194304 | tf_op jit(solution)/shard_map/adjoint/pallas_call | solution.py:170
  116.5 4.6 %adjoint.5.one_ref = bf16[2,16,64,128]{3,2,1,0:T(8,128)(2,1)} custom-call(s32[4]{0:T(128)S(1)} %pad_add_fusion.m, bf16[2,16,2,128,128]{4,3,2,1,0:T(8,128)(2,1)S(1)} %get-tuple-element.102.near_ref, bf16[2,16,2,128,128]{4,3,2,1,0:T(8,128)(2,1)} %collective-permute-done.10.far_ref, bf16[16,64,256]{2,1,0:T(8,128)(2,1)S(1)} %bitcast.104, ...), custom_call_target="tpu_custom_call" | custom-call | flops 536870912 | bytes 4194304 | tf_op jit(solution)/shard_map/adjoint/pallas_call | solution.py:170
  126.9 5.1 %forward.6 = (bf16[16,64,256]{2,1,0:T(8,128)(2,1)}, f32[16,64,256]{2,1,0:T(8,128)S(1)}) custom-call(s32[4]{0:T(128)S(1)} %pad_add_fusion.m, bf16[2,16,2,128,128]{4,3,2,1,0:T(8,128)(2,1)S(1)} %copy-done.2, bf16[2,16,2,128,128]{4,3,2,1,0:T(8,128)(2,1)} %collective-permute-done.4.far_ref, bf16[2,16,64,128]{3,2,1,0:T(8,128)(2,1)} %adjoint.4.one_ref, ...), custom_call_target="tpu_custom_call" | custom-call | flops 536870912 | bytes 4194304 | tf_op jit(solution)/shard_map/forward/pallas_call | solution.py:116
  132.1 2.0 collective-permute-done.30.two_ref
  134.1 5.2 %forward.7 = (bf16[16,64,256]{2,1,0:T(8,128)(2,1)}, f32[16,64,256]{2,1,0:T(8,128)S(1)}) custom-call(s32[4]{0:T(128)S(1)} %pad_add_fusion.m, bf16[2,16,2,128,128]{4,3,2,1,0:T(8,128)(2,1)S(1)} %get-tuple-element.102.near_ref, bf16[2,16,2,128,128]{4,3,2,1,0:T(8,128)(2,1)} %collective-permute-done.10.far_ref, bf16[2,16,64,128]{3,2,1,0:T(8,128)(2,1)} %adjoint.5.one_ref, ...), custom_call_target="tpu_custom_call" | custom-call | flops 536870912 | bytes 4194304 | tf_op jit(solution)/shard_map/forward/pallas_call | solution.py:116
  146.1 7.7 %collective-permute-done.17 = f32[1,128]{1,0:T(1,128)S(1)} collective-permute-done((f32[1,128]{1,0:T(1,128)S(1)}, f32[1,128]{1,0:T(1,128)S(1)}, u32[]{:S(2)}, u32[]{:S(2)}) %collective-permute-start.17) | collective-permute-done | bytes 544 | tf_op jit(solution)/shard_map/ppermute | solution.py:265
  155.0 2.4 collective-permute-done.18
  157.3 4.1 %collective-permute-start.19 = (f32[1,128]{1,0:T(1,128)S(1)}, f32[1,128]{1,0:T(1,128)S(1)}, u32[]{:S(2)}, u32[]{:S(2)}) collective-permute-start(f32[1,128]{1,0:T(1,128)S(1)} %add.227), channel_id=1, source_target_pairs={{0,4},{1,5},{2,6},{3,7},{4,0},{5,1},{6,2},{7,3},{8,12},{9,13},{10,... | collective-permute-start | bytes 1544 | tf_op jit(solution)/shard_map/ppermute | solution.py:265
  167.7 1.8 split.6
  169.6 2.0 collective-permute-start.33
  171.6 2.9 %collective-permute-start.34 = (bf16[256,256]{1,0:T(8,128)(2,1)}, bf16[256,256]{1,0:T(8,128)(2,1)}, u32[]{:S(2)}, u32[]{:S(2)}) collective-permute-start(bf16[256,256]{1,0:T(8,128)(2,1)} %get-tuple-element.72), channel_id=1, source_target_pairs={{0,4},{1,5},{2,6},{3,7},{4,0},{5,1},{6,2},{7,3},{8,12},{9,13},{10,... | collective-permute-start | bytes 393224 | tf_op jit(solution)/shard_map/ppermute | solution.py:256
  181.8 3.8 %collective-permute-start.38 = (bf16[256,256]{1,0:T(8,128)(2,1)}, bf16[256,256]{1,0:T(8,128)(2,1)S(1)}, u32[]{:S(2)}, u32[]{:S(2)}) collective-permute-start(bf16[256,256]{1,0:T(8,128)(2,1)} %copy-done.16), channel_id=1, source_target_pairs={{0,4},{1,5},{2,6},{3,7},{4,0},{5,1},{6,2},{7,3},{8,12},{9,13},{10,... | collective-permute-start | bytes 393224 | tf_op jit(solution)/shard_map/ppermute | solution.py:256
  187.0 3.9 %collective-permute-start.47 = (bf16[256,256]{1,0:T(8,128)(2,1)S(1)}, bf16[256,256]{1,0:T(8,128)(2,1)S(1)}, u32[]{:S(2)}, u32[]{:S(2)}) collective-permute-start(bf16[256,256]{1,0:T(8,128)(2,1)S(1)} %get-tuple-element.93.refs_0_), channel_id=1, source_target_pairs={{0,6},{1,7},{2,4},{3,5},{4,2},{5,3},{6,0},{7,1},{8,14},{9,15},{10,... | collective-permute-start | bytes 393224 | tf_op jit(solution)/shard_map/ppermute | solution.py:256
  190.9 4.5 %collective-permute-start.46 = (bf16[256,256]{1,0:T(8,128)(2,1)S(1)}, bf16[256,256]{1,0:T(8,128)(2,1)S(1)}, u32[]{:S(2)}, u32[]{:S(2)}) collective-permute-start(bf16[256,256]{1,0:T(8,128)(2,1)S(1)} %get-tuple-element.93.refs_0_), channel_id=1, source_target_pairs={{0,4},{1,5},{2,6},{3,7},{4,0},{5,1},{6,2},{7,3},{8,12},{9,13},{10,... | collective-permute-start | bytes 393224 | tf_op jit(solution)/shard_map/ppermute | solution.py:256
  198.9 2.6 collective-permute-start.52
  201.4 4.8 %collective-permute-start.51 = (bf16[256,256]{1,0:T(8,128)(2,1)S(1)}, bf16[256,256]{1,0:T(8,128)(2,1)S(1)}, u32[]{:S(2)}, u32[]{:S(2)}) collective-permute-start(bf16[256,256]{1,0:T(8,128)(2,1)S(1)} %get-tuple-element.95.refs_0_), channel_id=1, source_target_pairs={{0,4},{1,5},{2,6},{3,7},{4,0},{5,1},{6,2},{7,3},{8,12},{9,13},{10,... | collective-permute-start | bytes 393224 | tf_op jit(solution)/shard_map/ppermute | solution.py:256
  206.2 2.0 collective-permute-start.50
  208.2 2.3 collective-permute-done.46.refs_2_
  213.6 2.0 collective-permute-done.51.refs_2_
  222.8 2.0 stack.55
  228.4 4.0 %adjoint.6 = (bf16[16,64,128]{2,1,0:T(8,128)(2,1)S(1)}, f32[16,64,128]{2,1,0:T(8,128)S(1)}) custom-call(s32[4]{0:T(128)S(1)} %pad_add_fusion.m, bf16[2,16,2,128,128]{4,3,2,1,0:T(8,128)(2,1)S(1)} %copy-done.3, bf16[2,16,2,128,128]{4,3,2,1,0:T(8,128)(2,1)} %collective-permute-done.4.far_ref, bf16[16,64,256]{2,1,0:T(8,128)(2,1)} %bitcast.43.own_ref, ...), custom_call_target="tpu_custom_call" | custom-call | flops 536870912 | bytes 4194304 | tf_op jit(solution)/shard_map/adjoint/pallas_call | solution.py:170
  234.3 2.9 %collective-permute-done.41 = f32[1,128]{1,0:T(1,128)S(1)} collective-permute-done((f32[1,128]{1,0:T(1,128)S(1)}, f32[1,128]{1,0:T(1,128)S(1)}, u32[]{:S(2)}, u32[]{:S(2)}) %collective-permute-start.41) | collective-permute-done | bytes 544 | tf_op jit(solution)/shard_map/ppermute | solution.py:265
  238.0 2.8 %collective-permute-done.42 = f32[1,128]{1,0:T(1,128)S(1)} collective-permute-done((f32[1,128]{1,0:T(1,128)S(1)}, f32[1,128]{1,0:T(1,128)S(1)}, u32[]{:S(2)}, u32[]{:S(2)}) %collective-permute-start.42) | collective-permute-done | bytes 544 | tf_op jit(solution)/shard_map/ppermute | solution.py:265
  240.8 2.6 collective-permute-start.43
  243.3 1.9 collective-permute-done.43
  246.1 2.6 collective-permute-done.44
  248.7 5.0 %adjoint.7 = (bf16[16,64,128]{2,1,0:T(8,128)(2,1)}, f32[16,64,128]{2,1,0:T(8,128)S(1)}) custom-call(s32[4]{0:T(128)S(1)} %pad_add_fusion.m, bf16[2,16,2,128,128]{4,3,2,1,0:T(8,128)(2,1)S(1)} %get-tuple-element.102.near_ref, bf16[2,16,2,128,128]{4,3,2,1,0:T(8,128)(2,1)} %collective-permute-done.10.far_ref, bf16[16,64,256]{2,1,0:T(8,128)(2,1)} %bitcast.45.own_ref, ...), custom_call_target="tpu_custom_call" | custom-call | flops 536870912 | bytes 4194304 | tf_op jit(solution)/shard_map/adjoint/pallas_call | solution.py:170
  264.2 2.0 fusion.4
  (189 shorter events, 80.3 us)
Async XLA Ops:
  12.7 13.0 %collective-permute-start.4 = (bf16[2,16,2,128,128]{4,3,2,1,0:T(8,128)(2,1)}, bf16[2,16,2,128,128]{4,3,2,1,0:T(8,128)(2,1)}, u32[]{:S(2)}, u32[]{:S(2)}) collective-permute-start(bf16[2,16,2,128,128]{4,3,2,1,0:T(8,128)(2,1)} %get-tuple-element.101), channel_id=1, source_target_pairs={{0,8},{8,0},{16,24},{24,16},{1,9},{9,1},{17,25},{25,17},{2,10},{10... | collective-permute-start | bytes 6291464 | tf_op jit(solution)/shard_map/ppermute | solution.py:247
  13.2 19.4 %collective-permute-start.10 = (bf16[2,16,2,128,128]{4,3,2,1,0:T(8,128)(2,1)}, bf16[2,16,2,128,128]{4,3,2,1,0:T(8,128)(2,1)}, u32[]{:S(2)}, u32[]{:S(2)}) collective-permute-start(bf16[2,16,2,128,128]{4,3,2,1,0:T(8,128)(2,1)} %get-tuple-element.104), channel_id=1, source_target_pairs={{0,8},{8,0},{16,24},{24,16},{1,9},{9,1},{17,25},{25,17},{2,10},{10... | collective-permute-start | bytes 6291464 | tf_op jit(solution)/shard_map/ppermute | solution.py:247
  13.2 5.0 %collective-permute-start = (f32[16,128]{1,0:T(8,128)S(1)}, f32[16,128]{1,0:T(8,128)S(1)}, u32[]{:S(2)}, u32[]{:S(2)}) collective-permute-start(f32[16,128]{1,0:T(8,128)S(1)} %copy-done.26), channel_id=1, source_target_pairs={{0,1},{1,0},{2,3},{3,2},{4,5},{5,4},{6,7},{7,6},{8,9},{9,8},{10,11... | collective-permute-start | bytes 24584 | tf_op jit(solution)/shard_map/ppermute | solution.py:270
  16.2 9.5 %collective-permute-start.5 = (bf16[16,64,128]{2,1,0:T(8,128)(2,1)}, bf16[16,64,128]{2,1,0:T(8,128)(2,1)}, u32[]{:S(2)}, u32[]{:S(2)}) collective-permute-start(bf16[16,64,128]{2,1,0:T(8,128)(2,1)} %bitcast.2), channel_id=1, source_target_pairs={{0,16},{8,24},{16,0},{24,8},{1,17},{9,25},{17,1},{25,9},{2,18},{10... | collective-permute-start | bytes 786440 | tf_op jit(solution)/shard_map/ppermute | solution.py:250
  17.7 14.9 %collective-permute-start.11 = (bf16[16,64,128]{2,1,0:T(8,128)(2,1)}, bf16[16,64,128]{2,1,0:T(8,128)(2,1)S(1)}, u32[]{:S(2)}, u32[]{:S(2)}) collective-permute-start(bf16[16,64,128]{2,1,0:T(8,128)(2,1)} %bitcast.3), channel_id=1, source_target_pairs={{0,16},{8,24},{16,0},{24,8},{1,17},{9,25},{17,1},{25,9},{2,18},{10... | collective-permute-start | bytes 786440 | tf_op jit(solution)/shard_map/ppermute | solution.py:250
  18.2 3.8 %collective-permute-start.1 = (f32[32,128]{1,0:T(8,128)S(1)}, f32[32,128]{1,0:T(8,128)S(1)}, u32[]{:S(2)}, u32[]{:S(2)}) collective-permute-start(f32[32,128]{1,0:T(8,128)S(1)} %pad_maximum_fusion.2), channel_id=1, source_target_pairs={{0,2},{1,3},{2,0},{3,1},{4,6},{5,7},{6,4},{7,5},{8,10},{9,11},{10,... | collective-permute-start | bytes 49160 | tf_op jit(solution)/shard_map/ppermute | solution.py:270
  32.5 15.2 %collective-permute-start.6 = (bf16[16,64,256]{2,1,0:T(8,128)(2,1)}, bf16[16,64,256]{2,1,0:T(8,128)(2,1)}, u32[]{:S(2)}, u32[]{:S(2)}) collective-permute-start(bf16[16,64,256]{2,1,0:T(8,128)(2,1)} %get-tuple-element.57), channel_id=1, source_target_pairs={{0,1},{1,0},{2,3},{3,2},{4,5},{5,4},{6,7},{7,6},{8,9},{9,8},{10,11... | collective-permute-start | bytes 1572872 | tf_op jit(solution)/shard_map/ppermute | solution.py:253
  38.5 17.0 %collective-permute-start.12 = (bf16[16,64,256]{2,1,0:T(8,128)(2,1)}, bf16[16,64,256]{2,1,0:T(8,128)(2,1)}, u32[]{:S(2)}, u32[]{:S(2)}) collective-permute-start(bf16[16,64,256]{2,1,0:T(8,128)(2,1)} %get-tuple-element.63), channel_id=1, source_target_pairs={{0,1},{1,0},{2,3},{3,2},{4,5},{5,4},{6,7},{7,6},{8,9},{9,8},{10,11... | collective-permute-start | bytes 1572872 | tf_op jit(solution)/shard_map/ppermute | solution.py:253
  40.5 4.8 %collective-permute-start.2 = (f32[64,128]{1,0:T(8,128)S(1)}, f32[64,128]{1,0:T(8,128)S(1)}, u32[]{:S(2)}, u32[]{:S(2)}) collective-permute-start(f32[64,128]{1,0:T(8,128)S(1)} %pad_maximum_fusion.1), channel_id=1, source_target_pairs={{0,4},{1,5},{2,6},{3,7},{4,0},{5,1},{6,2},{7,3},{8,12},{9,13},{10,... | collective-permute-start | bytes 98312 | tf_op jit(solution)/shard_map/ppermute | solution.py:270
  46.0 13.5 %collective-permute-start.3 = (f32[2,32,128]{2,1,0:T(8,128)}, f32[2,32,128]{2,1,0:T(8,128)}, u32[]{:S(2)}, u32[]{:S(2)}) collective-permute-start(f32[2,32,128]{2,1,0:T(8,128)} %get-tuple-element.113), channel_id=1, source_target_pairs={{0,8},{8,0},{16,24},{24,16},{1,9},{9,1},{17,25},{25,17},{2,10},{10... | collective-permute-start | bytes 98312 | tf_op jit(solution)/shard_map/ppermute | solution.py:247
  50.8 12.1 %collective-permute-start.7 = (bf16[256,256]{1,0:T(8,128)(2,1)}, bf16[256,256]{1,0:T(8,128)(2,1)}, u32[]{:S(2)}, u32[]{:S(2)}) collective-permute-start(bf16[256,256]{1,0:T(8,128)(2,1)} %get-tuple-element.59), channel_id=1, source_target_pairs={{0,2},{1,3},{2,0},{3,1},{4,6},{5,7},{6,4},{7,5},{8,10},{9,11},{10,... | collective-permute-start | bytes 393224 | tf_op jit(solution)/shard_map/ppermute | solution.py:256
  52.4 13.3 %collective-permute-start.8 = (bf16[256,256]{1,0:T(8,128)(2,1)}, bf16[256,256]{1,0:T(8,128)(2,1)}, u32[]{:S(2)}, u32[]{:S(2)}) collective-permute-start(bf16[256,256]{1,0:T(8,128)(2,1)} %get-tuple-element.60), channel_id=1, source_target_pairs={{0,4},{1,5},{2,6},{3,7},{4,0},{5,1},{6,2},{7,3},{8,12},{9,13},{10,... | collective-permute-start | bytes 393224 | tf_op jit(solution)/shard_map/ppermute | solution.py:256
  54.9 10.7 %collective-permute-start.9 = (bf16[256,256]{1,0:T(8,128)(2,1)S(1)}, bf16[256,256]{1,0:T(8,128)(2,1)}, u32[]{:S(2)}, u32[]{:S(2)}) collective-permute-start(bf16[256,256]{1,0:T(8,128)(2,1)S(1)} %get-tuple-element.61), channel_id=1, source_target_pairs={{0,6},{1,7},{2,4},{3,5},{4,2},{5,3},{6,0},{7,1},{8,14},{9,15},{10,... | collective-permute-start | bytes 393224 | tf_op jit(solution)/shard_map/ppermute | solution.py:256
  57.9 23.3 %collective-permute-start.13 = (bf16[256,256]{1,0:T(8,128)(2,1)S(1)}, bf16[256,256]{1,0:T(8,128)(2,1)S(1)}, u32[]{:S(2)}, u32[]{:S(2)}) collective-permute-start(bf16[256,256]{1,0:T(8,128)(2,1)S(1)} %get-tuple-element.65), channel_id=1, source_target_pairs={{0,2},{1,3},{2,0},{3,1},{4,6},{5,7},{6,4},{7,5},{8,10},{9,11},{10,... | collective-permute-start | bytes 393224 | tf_op jit(solution)/shard_map/ppermute | solution.py:256
  60.3 21.3 %collective-permute-start.14 = (bf16[256,256]{1,0:T(8,128)(2,1)S(1)}, bf16[256,256]{1,0:T(8,128)(2,1)S(1)}, u32[]{:S(2)}, u32[]{:S(2)}) collective-permute-start(bf16[256,256]{1,0:T(8,128)(2,1)S(1)} %get-tuple-element.66), channel_id=1, source_target_pairs={{0,4},{1,5},{2,6},{3,7},{4,0},{5,1},{6,2},{7,3},{8,12},{9,13},{10,... | collective-permute-start | bytes 393224 | tf_op jit(solution)/shard_map/ppermute | solution.py:256
  62.9 18.7 %collective-permute-start.15 = (bf16[256,256]{1,0:T(8,128)(2,1)S(1)}, bf16[256,256]{1,0:T(8,128)(2,1)S(1)}, u32[]{:S(2)}, u32[]{:S(2)}) collective-permute-start(bf16[256,256]{1,0:T(8,128)(2,1)S(1)} %get-tuple-element.67), channel_id=1, source_target_pairs={{0,6},{1,7},{2,4},{3,5},{4,2},{5,3},{6,0},{7,1},{8,14},{9,15},{10,... | collective-permute-start | bytes 393224 | tf_op jit(solution)/shard_map/ppermute | solution.py:256
  67.4 22.0 %collective-permute-start.23 = (bf16[256,256]{1,0:T(8,128)(2,1)S(1)}, bf16[256,256]{1,0:T(8,128)(2,1)S(1)}, u32[]{:S(2)}, u32[]{:S(2)}) collective-permute-start(bf16[256,256]{1,0:T(8,128)(2,1)S(1)} %fusion.6.refs_0_), channel_id=1, source_target_pairs={{0,6},{1,7},{2,4},{3,5},{4,2},{5,3},{6,0},{7,1},{8,14},{9,15},{10,... | collective-permute-start | bytes 393224 | tf_op jit(solution)/shard_map/ppermute | solution.py:256
  70.1 25.4 %collective-permute-start.22 = (bf16[256,256]{1,0:T(8,128)(2,1)S(1)}, bf16[256,256]{1,0:T(8,128)(2,1)S(1)}, u32[]{:S(2)}, u32[]{:S(2)}) collective-permute-start(bf16[256,256]{1,0:T(8,128)(2,1)S(1)} %fusion.6.refs_0_), channel_id=1, source_target_pairs={{0,4},{1,5},{2,6},{3,7},{4,0},{5,1},{6,2},{7,3},{8,12},{9,13},{10,... | collective-permute-start | bytes 393224 | tf_op jit(solution)/shard_map/ppermute | solution.py:256
  81.2 14.3 %collective-permute-start.21 = (bf16[256,256]{1,0:T(8,128)(2,1)S(1)}, bf16[256,256]{1,0:T(8,128)(2,1)S(1)}, u32[]{:S(2)}, u32[]{:S(2)}) collective-permute-start(bf16[256,256]{1,0:T(8,128)(2,1)S(1)} %fusion.6.refs_0_), channel_id=1, source_target_pairs={{0,2},{1,3},{2,0},{3,1},{4,6},{5,7},{6,4},{7,5},{8,10},{9,11},{10,... | collective-permute-start | bytes 393224 | tf_op jit(solution)/shard_map/ppermute | solution.py:256
  83.0 13.6 %collective-permute-start.28 = (bf16[256,256]{1,0:T(8,128)(2,1)S(1)}, bf16[256,256]{1,0:T(8,128)(2,1)S(1)}, u32[]{:S(2)}, u32[]{:S(2)}) collective-permute-start(bf16[256,256]{1,0:T(8,128)(2,1)S(1)} %fusion.8.refs_0_), channel_id=1, source_target_pairs={{0,6},{1,7},{2,4},{3,5},{4,2},{5,3},{6,0},{7,1},{8,14},{9,15},{10,... | collective-permute-start | bytes 393224 | tf_op jit(solution)/shard_map/ppermute | solution.py:256
  85.3 14.4 %collective-permute-start.27 = (bf16[256,256]{1,0:T(8,128)(2,1)S(1)}, bf16[256,256]{1,0:T(8,128)(2,1)S(1)}, u32[]{:S(2)}, u32[]{:S(2)}) collective-permute-start(bf16[256,256]{1,0:T(8,128)(2,1)S(1)} %fusion.8.refs_0_), channel_id=1, source_target_pairs={{0,4},{1,5},{2,6},{3,7},{4,0},{5,1},{6,2},{7,3},{8,12},{9,13},{10,... | collective-permute-start | bytes 393224 | tf_op jit(solution)/shard_map/ppermute | solution.py:256
  89.5 10.3 %collective-permute-start.26 = (bf16[256,256]{1,0:T(8,128)(2,1)S(1)}, bf16[256,256]{1,0:T(8,128)(2,1)S(1)}, u32[]{:S(2)}, u32[]{:S(2)}) collective-permute-start(bf16[256,256]{1,0:T(8,128)(2,1)S(1)} %fusion.8.refs_0_), channel_id=1, source_target_pairs={{0,2},{1,3},{2,0},{3,1},{4,6},{5,7},{6,4},{7,5},{8,10},{9,11},{10,... | collective-permute-start | bytes 393224 | tf_op jit(solution)/shard_map/ppermute | solution.py:256
  96.0 12.7 %collective-permute-start.24 = (bf16[16,64,256]{2,1,0:T(8,128)(2,1)S(1)}, bf16[16,64,256]{2,1,0:T(8,128)(2,1)S(1)}, u32[]{:S(2)}, u32[]{:S(2)}) collective-permute-start(bf16[16,64,256]{2,1,0:T(8,128)(2,1)S(1)} %bitcast.101), channel_id=1, source_target_pairs={{0,1},{1,0},{2,3},{3,2},{4,5},{5,4},{6,7},{7,6},{8,9},{9,8},{10,11... | collective-permute-start | bytes 1572872 | tf_op jit(solution)/shard_map/ppermute | solution.py:253
  100.3 16.2 %collective-permute-start.29 = (bf16[16,64,256]{2,1,0:T(8,128)(2,1)S(1)}, bf16[16,64,256]{2,1,0:T(8,128)(2,1)S(1)}, u32[]{:S(2)}, u32[]{:S(2)}) collective-permute-start(bf16[16,64,256]{2,1,0:T(8,128)(2,1)S(1)} %bitcast.103), channel_id=1, source_target_pairs={{0,1},{1,0},{2,3},{3,2},{4,5},{5,4},{6,7},{7,6},{8,9},{9,8},{10,11... | collective-permute-start | bytes 1572872 | tf_op jit(solution)/shard_map/ppermute | solution.py:253
  113.3 11.9 %collective-permute-start.25 = (bf16[2,16,64,128]{3,2,1,0:T(8,128)(2,1)}, bf16[2,16,64,128]{3,2,1,0:T(8,128)(2,1)}, u32[]{:S(2)}, u32[]{:S(2)}) collective-permute-start(bf16[2,16,64,128]{3,2,1,0:T(8,128)(2,1)} %adjoint.4.one_ref), channel_id=1, source_target_pairs={{0,16},{8,24},{16,0},{24,8},{1,17},{9,25},{17,1},{25,9},{2,18},{10... | collective-permute-start | bytes 1572872 | tf_op jit(solution)/shard_map/ppermute | solution.py:250
  121.2 12.9 %collective-permute-start.30 = (bf16[2,16,64,128]{3,2,1,0:T(8,128)(2,1)}, bf16[2,16,64,128]{3,2,1,0:T(8,128)(2,1)}, u32[]{:S(2)}, u32[]{:S(2)}) collective-permute-start(bf16[2,16,64,128]{3,2,1,0:T(8,128)(2,1)} %adjoint.5.one_ref), channel_id=1, source_target_pairs={{0,16},{8,24},{16,0},{24,8},{1,17},{9,25},{17,1},{25,9},{2,18},{10... | collective-permute-start | bytes 1572872 | tf_op jit(solution)/shard_map/ppermute | solution.py:250
  132.0 34.5 %collective-permute-start.32 = (bf16[16,64,256]{2,1,0:T(8,128)(2,1)}, bf16[16,64,256]{2,1,0:T(8,128)(2,1)}, u32[]{:S(2)}, u32[]{:S(2)}) collective-permute-start(bf16[16,64,256]{2,1,0:T(8,128)(2,1)} %get-tuple-element.69), channel_id=1, source_target_pairs={{0,1},{1,0},{2,3},{3,2},{4,5},{5,4},{6,7},{7,6},{8,9},{9,8},{10,11... | collective-permute-start | bytes 1572872 | tf_op jit(solution)/shard_map/ppermute | solution.py:253
  140.2 34.3 %collective-permute-start.36 = (bf16[16,64,256]{2,1,0:T(8,128)(2,1)}, bf16[16,64,256]{2,1,0:T(8,128)(2,1)}, u32[]{:S(2)}, u32[]{:S(2)}) collective-permute-start(bf16[16,64,256]{2,1,0:T(8,128)(2,1)} %get-tuple-element.75), channel_id=1, source_target_pairs={{0,1},{1,0},{2,3},{3,2},{4,5},{5,4},{6,7},{7,6},{8,9},{9,8},{10,11... | collective-permute-start | bytes 1572872 | tf_op jit(solution)/shard_map/ppermute | solution.py:253
  144.5 9.3 %collective-permute-start.17 = (f32[1,128]{1,0:T(1,128)S(1)}, f32[1,128]{1,0:T(1,128)S(1)}, u32[]{:S(2)}, u32[]{:S(2)}) collective-permute-start(f32[1,128]{1,0:T(1,128)S(1)} %add.225), channel_id=1, source_target_pairs={{0,1},{1,0},{2,3},{3,2},{4,5},{5,4},{6,7},{7,6},{8,9},{9,8},{10,11... | collective-permute-start | bytes 1544 | tf_op jit(solution)/shard_map/ppermute | solution.py:265
  157.3 5.6 %collective-permute-start.19 = (f32[1,128]{1,0:T(1,128)S(1)}, f32[1,128]{1,0:T(1,128)S(1)}, u32[]{:S(2)}, u32[]{:S(2)}) collective-permute-start(f32[1,128]{1,0:T(1,128)S(1)} %add.227), channel_id=1, source_target_pairs={{0,4},{1,5},{2,6},{3,7},{4,0},{5,1},{6,2},{7,3},{8,12},{9,13},{10,... | collective-permute-start | bytes 1544 | tf_op jit(solution)/shard_map/ppermute | solution.py:265
  169.6 16.1 %collective-permute-start.33 = (bf16[256,256]{1,0:T(8,128)(2,1)}, bf16[256,256]{1,0:T(8,128)(2,1)}, u32[]{:S(2)}, u32[]{:S(2)}) collective-permute-start(bf16[256,256]{1,0:T(8,128)(2,1)} %get-tuple-element.71), channel_id=1, source_target_pairs={{0,2},{1,3},{2,0},{3,1},{4,6},{5,7},{6,4},{7,5},{8,10},{9,11},{10,... | collective-permute-start | bytes 393224 | tf_op jit(solution)/shard_map/ppermute | solution.py:256
  171.6 14.0 %collective-permute-start.34 = (bf16[256,256]{1,0:T(8,128)(2,1)}, bf16[256,256]{1,0:T(8,128)(2,1)}, u32[]{:S(2)}, u32[]{:S(2)}) collective-permute-start(bf16[256,256]{1,0:T(8,128)(2,1)} %get-tuple-element.72), channel_id=1, source_target_pairs={{0,4},{1,5},{2,6},{3,7},{4,0},{5,1},{6,2},{7,3},{8,12},{9,13},{10,... | collective-permute-start | bytes 393224 | tf_op jit(solution)/shard_map/ppermute | solution.py:256
  174.5 11.1 %collective-permute-start.35 = (bf16[256,256]{1,0:T(8,128)(2,1)}, bf16[256,256]{1,0:T(8,128)(2,1)}, u32[]{:S(2)}, u32[]{:S(2)}) collective-permute-start(bf16[256,256]{1,0:T(8,128)(2,1)} %get-tuple-element.73), channel_id=1, source_target_pairs={{0,6},{1,7},{2,4},{3,5},{4,2},{5,3},{6,0},{7,1},{8,14},{9,15},{10,... | collective-permute-start | bytes 393224 | tf_op jit(solution)/shard_map/ppermute | solution.py:256
  177.0 18.4 %collective-permute-start.37 = (bf16[256,256]{1,0:T(8,128)(2,1)}, bf16[256,256]{1,0:T(8,128)(2,1)}, u32[]{:S(2)}, u32[]{:S(2)}) collective-permute-start(bf16[256,256]{1,0:T(8,128)(2,1)} %get-tuple-element.77), channel_id=1, source_target_pairs={{0,2},{1,3},{2,0},{3,1},{4,6},{5,7},{6,4},{7,5},{8,10},{9,11},{10,... | collective-permute-start | bytes 393224 | tf_op jit(solution)/shard_map/ppermute | solution.py:256
  181.8 16.0 %collective-permute-start.38 = (bf16[256,256]{1,0:T(8,128)(2,1)}, bf16[256,256]{1,0:T(8,128)(2,1)S(1)}, u32[]{:S(2)}, u32[]{:S(2)}) collective-permute-start(bf16[256,256]{1,0:T(8,128)(2,1)} %copy-done.16), channel_id=1, source_target_pairs={{0,4},{1,5},{2,6},{3,7},{4,0},{5,1},{6,2},{7,3},{8,12},{9,13},{10,... | collective-permute-start | bytes 393224 | tf_op jit(solution)/shard_map/ppermute | solution.py:256
  185.6 12.2 %collective-permute-start.39 = (bf16[256,256]{1,0:T(8,128)(2,1)S(1)}, bf16[256,256]{1,0:T(8,128)(2,1)S(1)}, u32[]{:S(2)}, u32[]{:S(2)}) collective-permute-start(bf16[256,256]{1,0:T(8,128)(2,1)S(1)} %get-tuple-element.79), channel_id=1, source_target_pairs={{0,6},{1,7},{2,4},{3,5},{4,2},{5,3},{6,0},{7,1},{8,14},{9,15},{10,... | collective-permute-start | bytes 393224 | tf_op jit(solution)/shard_map/ppermute | solution.py:256
  187.0 19.2 %collective-permute-start.47 = (bf16[256,256]{1,0:T(8,128)(2,1)S(1)}, bf16[256,256]{1,0:T(8,128)(2,1)S(1)}, u32[]{:S(2)}, u32[]{:S(2)}) collective-permute-start(bf16[256,256]{1,0:T(8,128)(2,1)S(1)} %get-tuple-element.93.refs_0_), channel_id=1, source_target_pairs={{0,6},{1,7},{2,4},{3,5},{4,2},{5,3},{6,0},{7,1},{8,14},{9,15},{10,... | collective-permute-start | bytes 393224 | tf_op jit(solution)/shard_map/ppermute | solution.py:256
  190.9 19.7 %collective-permute-start.46 = (bf16[256,256]{1,0:T(8,128)(2,1)S(1)}, bf16[256,256]{1,0:T(8,128)(2,1)S(1)}, u32[]{:S(2)}, u32[]{:S(2)}) collective-permute-start(bf16[256,256]{1,0:T(8,128)(2,1)S(1)} %get-tuple-element.93.refs_0_), channel_id=1, source_target_pairs={{0,4},{1,5},{2,6},{3,7},{4,0},{5,1},{6,2},{7,3},{8,12},{9,13},{10,... | collective-permute-start | bytes 393224 | tf_op jit(solution)/shard_map/ppermute | solution.py:256
  195.4 15.1 %collective-permute-start.45 = (bf16[256,256]{1,0:T(8,128)(2,1)S(1)}, bf16[256,256]{1,0:T(8,128)(2,1)S(1)}, u32[]{:S(2)}, u32[]{:S(2)}) collective-permute-start(bf16[256,256]{1,0:T(8,128)(2,1)S(1)} %get-tuple-element.93.refs_0_), channel_id=1, source_target_pairs={{0,2},{1,3},{2,0},{3,1},{4,6},{5,7},{6,4},{7,5},{8,10},{9,11},{10,... | collective-permute-start | bytes 393224 | tf_op jit(solution)/shard_map/ppermute | solution.py:256
  198.9 14.7 %collective-permute-start.52 = (bf16[256,256]{1,0:T(8,128)(2,1)S(1)}, bf16[256,256]{1,0:T(8,128)(2,1)S(1)}, u32[]{:S(2)}, u32[]{:S(2)}) collective-permute-start(bf16[256,256]{1,0:T(8,128)(2,1)S(1)} %get-tuple-element.95.refs_0_), channel_id=1, source_target_pairs={{0,6},{1,7},{2,4},{3,5},{4,2},{5,3},{6,0},{7,1},{8,14},{9,15},{10,... | collective-permute-start | bytes 393224 | tf_op jit(solution)/shard_map/ppermute | solution.py:256
  201.4 14.2 %collective-permute-start.51 = (bf16[256,256]{1,0:T(8,128)(2,1)S(1)}, bf16[256,256]{1,0:T(8,128)(2,1)S(1)}, u32[]{:S(2)}, u32[]{:S(2)}) collective-permute-start(bf16[256,256]{1,0:T(8,128)(2,1)S(1)} %get-tuple-element.95.refs_0_), channel_id=1, source_target_pairs={{0,4},{1,5},{2,6},{3,7},{4,0},{5,1},{6,2},{7,3},{8,12},{9,13},{10,... | collective-permute-start | bytes 393224 | tf_op jit(solution)/shard_map/ppermute | solution.py:256
  206.2 9.4 %collective-permute-start.50 = (bf16[256,256]{1,0:T(8,128)(2,1)S(1)}, bf16[256,256]{1,0:T(8,128)(2,1)S(1)}, u32[]{:S(2)}, u32[]{:S(2)}) collective-permute-start(bf16[256,256]{1,0:T(8,128)(2,1)S(1)} %get-tuple-element.95.refs_0_), channel_id=1, source_target_pairs={{0,2},{1,3},{2,0},{3,1},{4,6},{5,7},{6,4},{7,5},{8,10},{9,11},{10,... | collective-permute-start | bytes 393224 | tf_op jit(solution)/shard_map/ppermute | solution.py:256
  211.9 14.9 %collective-permute-start.48 = (bf16[16,64,256]{2,1,0:T(8,128)(2,1)}, bf16[16,64,256]{2,1,0:T(8,128)(2,1)}, u32[]{:S(2)}, u32[]{:S(2)}) collective-permute-start(bf16[16,64,256]{2,1,0:T(8,128)(2,1)} %bitcast.43.own_ref), channel_id=1, source_target_pairs={{0,1},{1,0},{2,3},{3,2},{4,5},{5,4},{6,7},{7,6},{8,9},{9,8},{10,11... | collective-permute-start | bytes 1572872 | tf_op jit(solution)/shard_map/ppermute | solution.py:253
  217.0 31.7 %collective-permute-start.53 = (bf16[16,64,256]{2,1,0:T(8,128)(2,1)}, bf16[16,64,256]{2,1,0:T(8,128)(2,1)}, u32[]{:S(2)}, u32[]{:S(2)}) collective-permute-start(bf16[16,64,256]{2,1,0:T(8,128)(2,1)} %bitcast.45.own_ref), channel_id=1, source_target_pairs={{0,1},{1,0},{2,3},{3,2},{4,5},{5,4},{6,7},{7,6},{8,9},{9,8},{10,11... | collective-permute-start | bytes 1572872 | tf_op jit(solution)/shard_map/ppermute | solution.py:253
  225.5 8.1 %collective-permute-start.40 = (f32[1,128]{1,0:T(1,128)S(1)}, f32[1,128]{1,0:T(1,128)S(1)}, u32[]{:S(2)}, u32[]{:S(2)}) collective-permute-start(f32[1,128]{1,0:T(1,128)S(1)} %scatter.14), channel_id=1, source_target_pairs={{0,8},{8,0},{16,24},{24,16},{1,9},{9,1},{17,25},{25,17},{2,10},{10... | collective-permute-start | bytes 1544 | tf_op jit(solution)/shard_map/ppermute | solution.py:247
  232.4 28.7 %collective-permute-start.49 = (bf16[16,64,128]{2,1,0:T(8,128)(2,1)S(1)}, bf16[16,64,128]{2,1,0:T(8,128)(2,1)}, u32[]{:S(2)}, u32[]{:S(2)}) collective-permute-start(bf16[16,64,128]{2,1,0:T(8,128)(2,1)S(1)} %get-tuple-element.81), channel_id=1, source_target_pairs={{0,16},{8,24},{16,0},{24,8},{1,17},{9,25},{17,1},{25,9},{2,18},{10... | collective-permute-start | bytes 786440 | tf_op jit(solution)/shard_map/ppermute | solution.py:250
  240.8 4.4 %collective-permute-start.43 = (f32[1,128]{1,0:T(1,128)S(1)}, f32[1,128]{1,0:T(1,128)S(1)}, u32[]{:S(2)}, u32[]{:S(2)}) collective-permute-start(f32[1,128]{1,0:T(1,128)S(1)} %add.245), channel_id=1, source_target_pairs={{0,4},{1,5},{2,6},{3,7},{4,0},{5,1},{6,2},{7,3},{8,12},{9,13},{10,... | collective-permute-start | bytes 1544 | tf_op jit(solution)/shard_map/ppermute | solution.py:265
  254.5 7.8 %collective-permute-start.54 = (bf16[16,64,128]{2,1,0:T(8,128)(2,1)}, bf16[16,64,128]{2,1,0:T(8,128)(2,1)S(1)}, u32[]{:S(2)}, u32[]{:S(2)}) collective-permute-start(bf16[16,64,128]{2,1,0:T(8,128)(2,1)} %get-tuple-element.83), channel_id=1, source_target_pairs={{0,16},{8,24},{16,0},{24,8},{1,17},{9,25},{17,1},{25,9},{2,18},{10... | collective-permute-start | bytes 786440 | tf_op jit(solution)/shard_map/ppermute | solution.py:250
  (37 other events, 340.7 us)
where the time goes:
time: 268 us; the launch traced here: 266 us
  starting transfers between devices  93.2 us (35%)
  waiting for transfers between devices  61.4 us (23%)
  Pallas kernels  49.2 us (18%)
  local copies, waits for them, and re-layouts  28.5 us (11%)
  other arithmetic  22.3 us (8%)
  between operations  11.6 us (4%)
    ppermute x24, starting transfers between devices, to_group(): return lax.ppermute(array, 'src', [(j, j ^ 2 * d) for j in range(n_src)])  58.6 us
    pallas_call x4, Pallas kernels, forward_call(): pl.pallas_call(kernel, grid_spec=pltpu.PrefetchScalarGridSpec(num_scalar_...  20.5 us
    pallas_call x4, Pallas kernels, adjoint_call(): pl.pallas_call(kernel, grid_spec=pltpu.PrefetchScalarGridSpec(num_scalar_...  18.2 us
    ppermute x6, waiting for transfers between devices, total(): lax.ppermute(sums, 'src', [(j, j ^ bit) for j in range(n_src)])  17.6 us
    ppermute x24, waiting for transfers between devices, to_group(): return lax.ppermute(array, 'src', [(j, j ^ 2 * d) for j in range(n_src)])  15.3 us
    unnamed x60, local copies, waits for them, and re-layouts  13.3 us
    ppermute x8, waiting for transfers between devices, to_half(): return lax.ppermute(array, 'src', [(j, j ^ 1) for j in range(n_src)])  12.8 us
    ppermute x9, starting transfers between devices, to_pair(): return lax.ppermute(array, 'sens', [(i, i ^ 2) for i in range(n_sens)])  11 us
  transfers between devices with their start and end apart: 55, of which 24 were waited for; matrix products, arithmetic and copies ran while one was open for 8% of the time, Pallas kernels for 18%

commit v1 on v0

--- a/solution.py
+++ b/solution.py
@@ -124,7 +124,7 @@
                 pl.BlockSpec(out, lambda p, t, m: (jnp.where(p == 0, 0, t), 0, 0)),
             ],
         ),
-        out_shape=[jax.ShapeDtypeStruct(shape, BF16), jax.ShapeDtypeStruct(shape, F32)],
+        out_shape=[jax.ShapeDtypeStruct(shape, BF16)] * 2,
         cost_estimate=cost(plan.flops, 16 * plan.part * plan.sensors * plan.sources),
         compiler_params=pltpu.CompilerParams(vmem_limit_bytes=KERNEL_BYTES),
         name="forward",
@@ -187,61 +187,56 @@
     )(meta, near, far, *halves)
 
 
-def split_call(plan, meta, keep, got):
-    piece, groups = plan.piece, plan.groups
-    width = keep.shape[-1]
-
-    def kernel(m, keep_ref, got_ref, mine_ref, *sends):
-        for d in range(groups):
-            place = pl.ds(pl.multiple_of((m[3] ^ d) * piece, piece), piece)
-            total = keep_ref[place] + got_ref[place].astype(F32)
-            if d == 0:
-                mine_ref[...] = total
-            else:
-                sends[d - 1][...] = total.astype(BF16)
+def fold_call(plan, level, meta, keep, got):
+    height, width = keep.shape
+    cut = height // 2
+
+    def kernel(m, keep_ref, got_ref, send_ref, own_ref):
+        bit = (m[3] >> level) & 1
+        for out_ref, side in ((send_ref, 1 - bit), (own_ref, bit)):
+            place = pl.ds(pl.multiple_of(side * cut, cut), cut)
+            out_ref[...] = (keep_ref[place].astype(F32) + got_ref[place].astype(F32)).astype(BF16)
 
     whole = pl.BlockSpec(memory_space=pltpu.VMEM)
     return pl.pallas_call(
         kernel,
         in_specs=[pl.BlockSpec(memory_space=pltpu.SMEM), whole, whole],
-        out_specs=[whole] * groups,
-        out_shape=[jax.ShapeDtypeStruct((piece, width), F32)]
-        + [jax.ShapeDtypeStruct((piece, width), BF16)] * (groups - 1),
-        cost_estimate=cost(groups * piece * width, groups * piece * width * 8),
+        out_specs=[whole] * 2,
+        out_shape=[jax.ShapeDtypeStruct((cut, width), BF16)] * 2,
+        cost_estimate=cost(height * width, height * width * 6),
         compiler_params=pltpu.CompilerParams(vmem_limit_bytes=KERNEL_BYTES),
-        name="split",
-    )(meta, keep.reshape(-1, width), got.reshape(-1, width))
-
-
-def place_call(plan, meta, pieces):
-    piece, groups = plan.piece, plan.groups
-    width = pieces[0].shape[-1]
-
-    def kernel(m, *refs):
-        for d in range(groups):
-            place = pl.ds(pl.multiple_of((m[3] ^ d) * piece, piece), piece)
-            refs[groups][place] = refs[d][...]
+        name="fold",
+    )(meta, keep, got)
+
+
+def join_call(plan, level, meta, own, got):
+    height, width = own.shape
+
+    def kernel(m, own_ref, got_ref, out_ref):
+        bit = (m[3] >> level) & 1
+        for ref, side in ((own_ref, bit), (got_ref, 1 - bit)):
+            out_ref[pl.ds(pl.multiple_of(side * height, height), height)] = ref[...]
 
     whole = pl.BlockSpec(memory_space=pltpu.VMEM)
-    out = pl.pallas_call(
+    return pl.pallas_call(
         kernel,
-        in_specs=[pl.BlockSpec(memory_space=pltpu.SMEM)] + [whole] * groups,
+        in_specs=[pl.BlockSpec(memory_space=pltpu.SMEM), whole, whole],
         out_specs=whole,
-        out_shape=jax.ShapeDtypeStruct((groups * piece, width), BF16),
-        cost_estimate=cost(0, groups * piece * width * 4),
+        out_shape=jax.ShapeDtypeStruct((2 * height, width), BF16),
+        cost_estimate=cost(0, height * width * 8),
         compiler_params=pltpu.CompilerParams(vmem_limit_bytes=KERNEL_BYTES),
-        name="place",
-    )(meta, *pieces)
-    return out.reshape(plan.part, plan.rows, width)
+        name="join",
+    )(meta, own, got)
 
 
 def body(n_sens, n_src, operator, right_side, noise_weights, damping):
     plan = Plan(operator, right_side, n_sens, n_src, CHUNKS)
     sens, src = lax.axis_index("sens"), lax.axis_index("src")
-    pair, core = sens // 2, sens % 2
-    half, group = src % 2, src // 2
-    meta = jnp.stack([pair, core, half, group]).astype(jnp.int32)
+    pair, core, half = sens // 2, sens % 2, src % 2
+    meta = jnp.stack([pair, core, half, src]).astype(jnp.int32)
     part, rows, block = plan.part, plan.rows, plan.block
+    levels = range(n_src.bit_length() - 1)
+    chunks = range(plan.chunks)
 
     def to_core(array):
         return lax.ppermute(array, "sens", [(i, i ^ 1) for i in range(n_sens)])
@@ -249,117 +244,120 @@
     def to_pair(array):
         return lax.ppermute(array, "sens", [(i, i ^ 2) for i in range(n_sens)])
 
-    def to_half(array):
-        return lax.ppermute(array, "src", [(j, j ^ 1) for j in range(n_src)])
-
-    def to_group(array, d):
-        return lax.ppermute(array, "src", [(j, j ^ (2 * d)) for j in range(n_src)])
-
-    def src_bits():
-        return [2 ** bit for bit in range(n_src.bit_length() - 1)]
+    def to_src(array, level):
+        return lax.ppermute(array, "src", [(j, j ^ (1 << level)) for j in range(n_src)])
+
+    def lanes(array):
+        array = jnp.sum(array.reshape(-1, 8, array.shape[-1]), axis=0)
+        return jnp.sum(array.reshape(8, -1, 128), axis=1)
 
     def total(values):
-        sums = jnp.zeros((1, 128), F32).at[0, : len(values)].set(jnp.stack(values))
+        sums = jnp.concatenate(values, axis=0)
+        for level in levels:
+            sums = sums + to_src(sums, level)
+        sums = sums + to_pair(sums)
         sums = sums + to_core(sums)
-        for bit in src_bits():
-            sums = sums + lax.ppermute(sums, "src", [(j, j ^ bit) for j in range(n_src)])
-        return (sums + to_pair(sums))[0]
-
-    def all_weights(table):
-        for bit in src_bits():
-            other = lax.ppermute(table, "src", [(j, j ^ bit) for j in range(n_src)])
-            low = (src // bit) % 2 == 0
-            table = jnp.concatenate(
-                [jnp.where(low, table, other), jnp.where(low, other, table)], axis=0
-            )
-        return table
+        return jnp.sum(sums.reshape(len(values), -1), axis=1)
+
+    def double(table, level):
+        other = to_src(table, level)
+        low = (src >> level) % 2 == 0
+        return jnp.concatenate([jnp.where(low, table, other), jnp.where(low, other, table)], axis=0)
 
     whole = operator.reshape(plan.pairs, 2, block, 2, plan.sensors, plan.sources)
     start = right_side.reshape(block, rows, plan.sources)
-    chunks = range(plan.chunks)
-
-    sent_b = [start[k * part:(k + 1) * part].astype(BF16) for k in chunks]
-    got_b = [to_pair(sent) for sent in sent_b]
-    core, *_ = lax.optimization_barrier((core, *sent_b))
 
     def half_of(k, which):
         size = (plan.pairs, 1, part, 2, plan.sensors, plan.sources)
         cut = lax.dynamic_slice(whole, (0, which, k * part, 0, 0, 0), size)
         return cut.reshape(plan.pairs, part, 2, plan.sensors, plan.sources)
 
-    near, far = [], []
-    for k in chunks:
-        far.append(to_core(half_of(k, 1 - core)))
-        near.append(half_of(k, core))
-
-    weights = all_weights(noise_weights)
+    sent_b = [start[k * part:(k + 1) * part].astype(BF16) for k in chunks]
+    got_b = [to_pair(sent) for sent in sent_b]
+    other, *_ = lax.optimization_barrier((1 - core, *sent_b))
+    far = [to_core(half_of(k, other)) for k in chunks]
+    weights = double(noise_weights, 0)
+    core_late, _ = lax.optimization_barrier((core, weights))
+    near = [half_of(k, core_late) for k in chunks]
+
+    for level in levels[1:]:
+        weights = double(weights, level)
     weights = weights.reshape(plan.pairs, 2, block, plan.sensors)
     weights_near = lax.dynamic_index_in_dim(weights, core, 1, keepdims=False)
     weights_far = to_core(lax.dynamic_index_in_dim(weights, 1 - core, 1, keepdims=False))
     weights = jnp.concatenate([weights_near, weights_far], axis=-1)
     weights = lax.dynamic_index_in_dim(weights, pair ^ half, 0, keepdims=False)
     damping_row = jnp.where(half == 0, damping, to_pair(damping))
+    first_row = sum(((src >> level) & 1) * ((part * rows) >> level) for level in levels[1:])
     count = max(1, plan.piece // rows)
 
     def piece_of(k, table):
-        place = k * part + group * plan.piece // rows
-        cut = lax.dynamic_slice_in_dim(table, place, count, 0)
+        cut = lax.dynamic_slice_in_dim(table, k * part + first_row // rows, count, 0)
         return cut.reshape(count, 1, -1)
 
     def reduce_field(send, keep):
-        mine, *sends = split_call(plan, meta, keep, to_half(send))
-        for d, piece in enumerate(sends):
-            mine = mine + to_group(piece, d + 1).astype(F32)
+        keep, got = keep.reshape(part * rows, -1), to_src(send, 0).reshape(part * rows, -1)
+        for level in levels[1:]:
+            send, keep = fold_call(plan, level, meta, keep, got)
+            got = to_src(send, level)
+        mine = keep.astype(F32) + got.astype(F32)
         return mine.reshape(count, plan.piece // count, -1)
 
     def gather_field(weighted):
-        weighted = weighted.astype(BF16).reshape(plan.piece, -1)
-        pieces = [weighted] + [to_group(weighted, d) for d in range(1, plan.groups)]
-        own = place_call(plan, meta, pieces)
-        return own, to_half(own)
+        own = weighted.astype(BF16).reshape(plan.piece, -1)
+        for level in reversed(levels[1:]):
+            own = join_call(plan, level, meta, own, to_src(own, level))
+        own = own.reshape(part, rows, -1)
+        return own, to_src(own, 0)
 
     field, products = [], []
     for k in chunks:
         send, keep = forward_call(plan, k, meta, near[k], far[k], True, (start, got_b[k]))
         field.append(reduce_field(send, keep))
     scaled = [piece_of(k, weights) * field[k] for k in chunks]
+    damp = damping[:, None, None]
+    start_late, _ = lax.optimization_barrier((start, got_b[-1]))
+    sums = total([
+        lanes(start_late * start_late),
+        lanes(damp * start_late * start_late) + sum(lanes(scaled[k] * field[k]) for k in chunks),
+    ])
+    norm_0, curve_0 = sums[0], sums[1]
+    alpha_0 = norm_0 / curve_0
     for k in chunks:
         back = adjoint_call(plan, meta, near[k], far[k], gather_field(scaled[k]), False)
         products.append((back, to_pair(back)))
-    damp = damping[:, None, None]
-    norm, curve = jnp.sum(start * start), jnp.sum(damp * start * start)
-    for k in chunks:
-        curve = curve + jnp.sum(scaled[k] * field[k])
-    sums = total([norm, curve])
-    norm_0, curve_0 = sums[0], sums[1]
-    alpha_0 = norm_0 / curve_0
+    alpha_0, products[0] = lax.optimization_barrier((alpha_0, products[0]))
 
     image_0 = jnp.concatenate([mine[0].astype(F32) + got[1].astype(F32) for mine, got in products])
     image_0 = image_0 + damp * start
     residual = start - alpha_0 * image_0
-    values = [
-        jnp.sum(residual * residual),
-        jnp.sum(damp * residual * residual),
-        jnp.sum(damp * residual * start),
-    ]
-
-    square = cross = 0.0
-    final = []
+
+    new_scaled, square, cross = [], 0.0, 0.0
     for k in chunks:
         send, keep = forward_call(plan, k, meta, near[k], far[k], False, products[k])
         factor = 1.0 - alpha_0 * piece_of(k, damping_row)
         new_field = factor * field[k] - alpha_0 * reduce_field(send, keep)
-        new_scaled = piece_of(k, weights) * new_field
-        square = square + jnp.sum(new_scaled * new_field)
-        cross = cross + jnp.sum(new_scaled * field[k])
-        other, own = adjoint_call(plan, meta, near[k], far[k], gather_field(new_scaled), True)
-        final.append(own + to_pair(other).astype(F32))
-    sums = total(values + [square, cross])
+        new_scaled.append(piece_of(k, weights) * new_field)
+        square = square + lanes(new_scaled[k] * new_field)
+        cross = cross + lanes(new_scaled[k] * field[k])
+    damped = damp * residual
+    sums = total([
+        lanes(residual * residual),
+        lanes(damped * residual) + square,
+        lanes(damped * start) + cross,
+    ])
     norm_1 = sums[0]
     beta = norm_1 / norm_0
-    curve_1 = (sums[1] + sums[3]) + 2.0 * beta * (sums[2] + sums[4]) + beta * beta * curve_0
+    curve_1 = sums[1] + 2.0 * beta * sums[2] + beta * beta * curve_0
     alpha_1 = norm_1 / curve_1
 
+    final = []
+    for k in chunks:
+        halves = gather_field(new_scaled[k])
+        if k == plan.chunks - 1:
+            alpha_1, halves = lax.optimization_barrier((alpha_1, halves))
+        sent, own = adjoint_call(plan, meta, near[k], far[k], halves, True)
+        final.append(own + to_pair(sent).astype(F32))
     image_1 = jnp.concatenate(final) + damp * residual + beta * image_0
     solution = alpha_0 * start + alpha_1 * (residual + beta * start)
     residual = residual - alpha_1 * image_1

time: 268 us -> 278 us (1.037)
  waiting for transfers between devices: 61.4 us -> 97.9 us
  starting transfers between devices: 93.2 us -> 62.4 us
  Pallas kernels: 49.2 us -> 56.6 us
  between operations: 11.6 us -> 6.13 us
  local copies, waits for them, and re-layouts: 28.5 us -> 32.5 us
    ppermute x41 -> x33, starting transfers between devices: 81.6 us -> 51.2 us  [to_src(): lax.ppermute(array, 'src', [(j, j ^ 1 << level) for j in range(n_src)])]
    ppermute x41 -> x33, waiting for transfers between devices: 50 us -> 77.5 us  [to_src(): lax.ppermute(array, 'src', [(j, j ^ 1 << level) for j in range(n_src)])]
    pallas_call x8 -> x16, Pallas kernels: 10.5 us -> 19.2 us  [the longest x8 11.4 us: fold_call(): pl.pallas_call(kernel, in_specs=[pl.BlockSpec(memory_space=pltpu.SMEM), w...]
    ppermute x9, waiting for transfers between devices: 10.3 us -> 18.1 us  [to_pair(): return lax.ppermute(array, 'sens', [(i, i ^ 2) for i in range(n_sens)])]
    mul x0 -> x4, local copies, waits for them, and re-layouts: none -> 3.23 us  [the longest x2 2.02 us: body(): damp * start_late * start_late]
    mul x4 -> x8, local copies, waits for them, and re-layouts: 1.94 us -> 4.89 us  [body(): new_field = factor * field[k] - alpha_0 * reduce_field(send, keep)]
    unnamed x60 -> x78, local copies, waits for them, and re-layouts: 13.3 us -> 13.5 us
    reduce_sum x6 -> x17, other arithmetic: 7.97 us -> 8.03 us  [the longest x7 6.88 us: lanes(): array = jnp.sum(array.reshape(-1, 8, array.shape[-1]), axis=0)]
  transfers between devices with their start and end apart: 55 -> 47, of which waited for: 24 -> 27; matrix products, arithmetic and copies ran while one was open for 8% -> 11% of each run, Pallas kernels for 18% -> 21%
where the time goes in v1:
time: 278 us; the launch traced here: 276 us
  waiting for transfers between devices  97.9 us (35%)
  starting transfers between devices  62.4 us (22%)
  Pallas kernels  56.6 us (20%)
  local copies, waits for them, and re-layouts  32.5 us (12%)
  other arithmetic  20.5 us (7%)
  between operations  6.13 us (2%)
    ppermute x33, waiting for transfers between devices, to_src(): lax.ppermute(array, 'src', [(j, j ^ 1 << level) for j in range(n_src)])  77.5 us
    ppermute x33, starting transfers between devices, to_src(): lax.ppermute(array, 'src', [(j, j ^ 1 << level) for j in range(n_src)])  51.2 us
    pallas_call x4, Pallas kernels, forward_call(): pl.pallas_call(kernel, grid_spec=pltpu.PrefetchScalarGridSpec(num_scalar_...  20.5 us
    ppermute x9, waiting for transfers between devices, to_pair(): return lax.ppermute(array, 'sens', [(i, i ^ 2) for i in range(n_sens)])  18.1 us
    pallas_call x4, Pallas kernels, adjoint_call(): pl.pallas_call(kernel, grid_spec=pltpu.PrefetchScalarGridSpec(num_scalar_...  16.9 us
    unnamed x78, local copies, waits for them, and re-layouts  13.5 us
    pallas_call x8, Pallas kernels, fold_call(): pl.pallas_call(kernel, in_specs=[pl.BlockSpec(memory_space=pltpu.SMEM), w...  11.4 us
    ppermute x9, starting transfers between devices, to_pair(): return lax.ppermute(array, 'sens', [(i, i ^ 2) for i in range(n_sens)])  10.6 us
  transfers between devices with their start and end apart: 47, of which 27 were waited for; matrix products, arithmetic and copies ran while one was open for 11% of the time, Pallas kernels for 21%

profile of v1, /device:TPU:0, one launch (start us, length us, event | category | flops | bytes accessed | tf_op | source)
XLA Modules:
  0.0 275.9 jit_solution(17791776619304474682)
XLA Ops:
  0.6 3.0 %collective-permute-start.1 = (f32[16,128]{1,0:T(8,128)}, f32[16,128]{1,0:T(8,128)S(1)}, u32[]{:S(2)}, u32[]{:S(2)}) collective-permute-start(f32[16,128]{1,0:T(8,128)} %param.6), channel_id=1, source_target_pairs={{0,1},{1,0},{2,3},{3,2},{4,5},{5,4},{6,7},{7,6},{8,9},{9,8},{10,11... | collective-permute-start | bytes 24584 | tf_op jit(solution)/shard_map/ppermute | solution.py:248
  5.9 8.0 %dynamic-slice_bitcast_fusion.2 = (bf16[2,16,2,128,128]{4,3,2,1,0:T(8,128)(2,1)}, bf16[2,16,2,128,128]{4,3,2,1,0:T(8,128)(2,1)S(1)}, bf16[2,16,2,128,128]{4,3,2,1,0:T(8,128)(2,1)}, bf16[2,16,2,128,128]{4,3,2,1,0:T(8,128)(2,1)}) fusion(bf16[2,2,32,2,128,128]{5,4,3,2,1,0:T(8,128)(2,1)} %bitcast.138, s32[]{:T(128)S(6)} %select_n.137, s32[]{:T(128)S(6)} %select_n.136), kind=kLoop, calls=%fused_computation.2 | loop fusion | bytes 16777224 | tf_op jit(solution)/shard_map/reshape | solution.py:273
  18.3 5.6 %collective-permute-done.6.two_ref = bf16[16,64,128]{2,1,0:T(8,128)(2,1)} collective-permute-done((bf16[16,64,128]{2,1,0:T(8,128)(2,1)}, bf16[16,64,128]{2,1,0:T(8,128)(2,1)}, u32[]{:S(2)}, u32[]{:S(2)}) %collective-permute-start.6) | collective-permute-done | bytes 262176 | tf_op jit(solution)/shard_map/ppermute | solution.py:245
  25.5 5.2 %forward.4 = (bf16[16,64,256]{2,1,0:T(8,128)(2,1)}, bf16[16,64,256]{2,1,0:T(8,128)(2,1)S(1)}) custom-call(s32[4]{0:T(128)S(1)} %pad_add_fusion.m, bf16[2,16,2,128,128]{4,3,2,1,0:T(8,128)(2,1)S(1)} %copy-done, bf16[2,16,2,128,128]{4,3,2,1,0:T(8,128)(2,1)} %collective-permute-done.5.far_ref, f32[32,64,128]{2,1,0:T(8,128)S(1)} %bitcast.124, ...), custom_call_target="tpu_custom_call" | custom-call | flops 536870912 | bytes 4194304 | tf_op jit(solution)/shard_map/forward/pallas_call | solution.py:116
  32.4 5.0 %forward.5 = (bf16[16,64,256]{2,1,0:T(8,128)(2,1)}, bf16[16,64,256]{2,1,0:T(8,128)(2,1)S(1)}) custom-call(s32[4]{0:T(128)S(1)} %pad_add_fusion.m, bf16[2,16,2,128,128]{4,3,2,1,0:T(8,128)(2,1)S(1)} %get-tuple-element.84.near_ref, bf16[2,16,2,128,128]{4,3,2,1,0:T(8,128)(2,1)} %collective-permute-done.10.far_ref, f32[32,64,128]{2,1,0:T(8,128)S(1)} %bitcast.125, ...), custom_call_target="tpu_custom_call" | custom-call | flops 536870912 | bytes 4194304 | tf_op jit(solution)/shard_map/forward/pallas_call | solution.py:116
  38.6 2.8 %collective-permute-start.3 = (f32[64,128]{1,0:T(8,128)S(1)}, f32[64,128]{1,0:T(8,128)S(1)}, u32[]{:S(2)}, u32[]{:S(2)}) collective-permute-start(f32[64,128]{1,0:T(8,128)S(1)} %pad_maximum_fusion.2), channel_id=1, source_target_pairs={{0,4},{1,5},{2,6},{3,7},{4,0},{5,1},{6,2},{7,3},{8,12},{9,13},{10,... | collective-permute-start | bytes 98312 | tf_op jit(solution)/shard_map/ppermute | solution.py:248
  41.4 2.1 collective-permute-done.3
  43.5 2.5 collective-permute-done.7
  46.9 1.8 fold.8
  50.5 3.8 %collective-permute-done.11 = bf16[16,64,256]{2,1,0:T(8,128)(2,1)} collective-permute-done((bf16[16,64,256]{2,1,0:T(8,128)(2,1)}, bf16[16,64,256]{2,1,0:T(8,128)(2,1)}, u32[]{:S(2)}, u32[]{:S(2)}) %collective-permute-start.11) | collective-permute-done | bytes 524320 | tf_op jit(solution)/shard_map/ppermute | solution.py:248
  55.3 1.8 fold.10
  62.9 2.7 collective-permute-start.9
  67.6 1.9 collective-permute-start.13
  70.1 5.1 %collective-permute-done.9 = bf16[256,256]{1,0:T(8,128)(2,1)S(1)} collective-permute-done((bf16[256,256]{1,0:T(8,128)(2,1)S(1)}, bf16[256,256]{1,0:T(8,128)(2,1)S(1)}, u32[]{:S(2)}, u32[]{:S(2)}) %collective-permute-start.9) | collective-permute-done | bytes 131104 | tf_op jit(solution)/shard_map/ppermute | solution.py:248
  75.3 2.5 collective-permute-done.13
  79.1 6.3 %collective-permute-done.19.got_ref = bf16[256,256]{1,0:T(8,128)(2,1)S(1)} collective-permute-done((bf16[256,256]{1,0:T(8,128)(2,1)S(1)}, bf16[256,256]{1,0:T(8,128)(2,1)S(1)}, u32[]{:S(2)}, u32[]{:S(2)}) %collective-permute-start.19) | collective-permute-done | bytes 131104 | tf_op jit(solution)/shard_map/ppermute | solution.py:248
  86.6 2.3 collective-permute-start.20
  92.7 2.1 reduce_sum.206
  104.1 10.1 %collective-permute-done.21.got_ref = bf16[16,64,256]{2,1,0:T(8,128)(2,1)S(1)} collective-permute-done((bf16[16,64,256]{2,1,0:T(8,128)(2,1)S(1)}, bf16[16,64,256]{2,1,0:T(8,128)(2,1)S(1)}, u32[]{:S(2)}, u32[]{:S(2)}) %collective-permute-start.21) | collective-permute-done | bytes 524320 | tf_op jit(solution)/shard_map/ppermute | solution.py:248
  114.3 4.6 %adjoint.4.one_ref = bf16[2,16,64,128]{3,2,1,0:T(8,128)(2,1)} custom-call(s32[4]{0:T(128)S(1)} %pad_add_fusion.m, bf16[2,16,2,128,128]{4,3,2,1,0:T(8,128)(2,1)S(1)} %copy-done.1, bf16[2,16,2,128,128]{4,3,2,1,0:T(8,128)(2,1)} %collective-permute-done.5.far_ref, bf16[16,64,256]{2,1,0:T(8,128)(2,1)S(1)} %bitcast.129, ...), custom_call_target="tpu_custom_call" | custom-call | flops 536870912 | bytes 4194304 | tf_op jit(solution)/shard_map/adjoint/pallas_call | solution.py:170
  121.8 4.6 %adjoint.5.one_ref = bf16[2,16,64,128]{3,2,1,0:T(8,128)(2,1)} custom-call(s32[4]{0:T(128)S(1)} %pad_add_fusion.m, bf16[2,16,2,128,128]{4,3,2,1,0:T(8,128)(2,1)S(1)} %get-tuple-element.84.near_ref, bf16[2,16,2,128,128]{4,3,2,1,0:T(8,128)(2,1)} %collective-permute-done.10.far_ref, bf16[16,64,256]{2,1,0:T(8,128)(2,1)S(1)} %bitcast.131, ...), custom_call_target="tpu_custom_call" | custom-call | flops 536870912 | bytes 4194304 | tf_op jit(solution)/shard_map/adjoint/pallas_call | solution.py:170
  127.9 1.7 collective-permute-start.15
  129.7 1.9 collective-permute-done.15
  131.6 3.0 %collective-permute-start.16 = (f32[16,128]{1,0:T(8,128)S(1)}, f32[16,128]{1,0:T(8,128)S(1)}, u32[]{:S(2)}, u32[]{:S(2)}) collective-permute-start(f32[16,128]{1,0:T(8,128)S(1)} %add.201), channel_id=1, source_target_pairs={{0,4},{1,5},{2,6},{3,7},{4,0},{5,1},{6,2},{7,3},{8,12},{9,13},{10,... | collective-permute-start | bytes 24584 | tf_op jit(solution)/shard_map/ppermute | solution.py:248
  136.7 3.1 %collective-permute-done.17 = f32[16,128]{1,0:T(8,128)S(1)} collective-permute-done((f32[16,128]{1,0:T(8,128)S(1)}, f32[16,128]{1,0:T(8,128)S(1)}, u32[]{:S(2)}, u32[]{:S(2)}) %collective-permute-start.17) | collective-permute-done | bytes 8224 | tf_op jit(solution)/shard_map/ppermute | solution.py:245
  146.0 5.2 %forward.6 = (bf16[16,64,256]{2,1,0:T(8,128)(2,1)}, bf16[16,64,256]{2,1,0:T(8,128)(2,1)S(1)}) custom-call(s32[4]{0:T(128)S(1)} %pad_add_fusion.m, bf16[2,16,2,128,128]{4,3,2,1,0:T(8,128)(2,1)S(1)} %copy-done.2, bf16[2,16,2,128,128]{4,3,2,1,0:T(8,128)(2,1)} %collective-permute-done.5.far_ref, bf16[2,16,64,128]{3,2,1,0:T(8,128)(2,1)} %adjoint.4.one_ref, ...), custom_call_target="tpu_custom_call" | custom-call | flops 536870912 | bytes 4194304 | tf_op jit(solution)/shard_map/forward/pallas_call | solution.py:116
  152.7 5.2 %forward.7 = (bf16[16,64,256]{2,1,0:T(8,128)(2,1)}, bf16[16,64,256]{2,1,0:T(8,128)(2,1)S(1)}) custom-call(s32[4]{0:T(128)S(1)} %pad_add_fusion.m, bf16[2,16,2,128,128]{4,3,2,1,0:T(8,128)(2,1)S(1)} %get-tuple-element.84.near_ref, bf16[2,16,2,128,128]{4,3,2,1,0:T(8,128)(2,1)} %collective-permute-done.10.far_ref, bf16[2,16,64,128]{3,2,1,0:T(8,128)(2,1)} %adjoint.5.one_ref, ...), custom_call_target="tpu_custom_call" | custom-call | flops 536870912 | bytes 4194304 | tf_op jit(solution)/shard_map/forward/pallas_call | solution.py:116
  162.7 2.2 fusion.21
  167.3 1.8 fold.12
  171.5 5.2 %collective-permute-done.31 = bf16[16,64,256]{2,1,0:T(8,128)(2,1)} collective-permute-done((bf16[16,64,256]{2,1,0:T(8,128)(2,1)}, bf16[16,64,256]{2,1,0:T(8,128)(2,1)}, u32[]{:S(2)}, u32[]{:S(2)}) %collective-permute-start.31) | collective-permute-done | bytes 524320 | tf_op jit(solution)/shard_map/ppermute | solution.py:248
  176.7 1.8 fold.14
  180.9 2.1 fusion.22
  191.7 2.9 %collective-permute-start.30 = (bf16[256,256]{1,0:T(8,128)(2,1)S(1)}, bf16[256,256]{1,0:T(8,128)(2,1)S(1)}, u32[]{:S(2)}, u32[]{:S(2)}) collective-permute-start(bf16[256,256]{1,0:T(8,128)(2,1)S(1)} %get-tuple-element.62), channel_id=1, source_target_pairs={{0,4},{1,5},{2,6},{3,7},{4,0},{5,1},{6,2},{7,3},{8,12},{9,13},{10,... | collective-permute-start | bytes 393224 | tf_op jit(solution)/shard_map/ppermute | solution.py:248
  196.9 6.1 %collective-permute-done.30 = bf16[256,256]{1,0:T(8,128)(2,1)S(1)} collective-permute-done((bf16[256,256]{1,0:T(8,128)(2,1)S(1)}, bf16[256,256]{1,0:T(8,128)(2,1)S(1)}, u32[]{:S(2)}, u32[]{:S(2)}) %collective-permute-start.30) | collective-permute-done | bytes 131104 | tf_op jit(solution)/shard_map/ppermute | solution.py:248
  203.2 3.8 %collective-permute-done.33 = bf16[256,256]{1,0:T(8,128)(2,1)S(1)} collective-permute-done((bf16[256,256]{1,0:T(8,128)(2,1)S(1)}, bf16[256,256]{1,0:T(8,128)(2,1)S(1)}, u32[]{:S(2)}, u32[]{:S(2)}) %collective-permute-start.33) | collective-permute-done | bytes 131104 | tf_op jit(solution)/shard_map/ppermute | solution.py:248
  207.6 5.7 %collective-permute-done.42.got_ref = bf16[256,256]{1,0:T(8,128)(2,1)S(1)} collective-permute-done((bf16[256,256]{1,0:T(8,128)(2,1)S(1)}, bf16[256,256]{1,0:T(8,128)(2,1)S(1)}, u32[]{:S(2)}, u32[]{:S(2)}) %collective-permute-start.42) | collective-permute-done | bytes 131104 | tf_op jit(solution)/shard_map/ppermute | solution.py:248
  213.9 2.2 collective-permute-start.43
  216.7 2.0 collective-permute-start.40
  218.7 4.6 %collective-permute-done.43.got_ref = bf16[512,256]{1,0:T(8,128)(2,1)S(1)} collective-permute-done((bf16[512,256]{1,0:T(8,128)(2,1)S(1)}, bf16[512,256]{1,0:T(8,128)(2,1)S(1)}, u32[]{:S(2)}, u32[]{:S(2)}) %collective-permute-start.43) | collective-permute-done | bytes 262176 | tf_op jit(solution)/shard_map/ppermute | solution.py:248
  229.5 9.0 %collective-permute-done.34 = f32[24,128]{1,0:T(8,128)S(1)} collective-permute-done((f32[24,128]{1,0:T(8,128)S(1)}, f32[24,128]{1,0:T(8,128)S(1)}, u32[]{:S(2)}, u32[]{:S(2)}) %collective-permute-start.34) | collective-permute-done | bytes 12320 | tf_op jit(solution)/shard_map/ppermute | solution.py:248
  238.5 1.9 collective-permute-start.35
  240.4 1.8 collective-permute-done.35
  242.2 2.9 %collective-permute-start.36 = (f32[24,128]{1,0:T(8,128)S(1)}, f32[24,128]{1,0:T(8,128)S(1)}, u32[]{:S(2)}, u32[]{:S(2)}) collective-permute-start(f32[24,128]{1,0:T(8,128)S(1)} %add.217), channel_id=1, source_target_pairs={{0,4},{1,5},{2,6},{3,7},{4,0},{5,1},{6,2},{7,3},{8,12},{9,13},{10,... | collective-permute-start | bytes 36872 | tf_op jit(solution)/shard_map/ppermute | solution.py:248
  248.5 2.0 collective-permute-done.37
  250.6 3.7 %adjoint.6 = (bf16[16,64,128]{2,1,0:T(8,128)(2,1)S(1)}, f32[16,64,128]{2,1,0:T(8,128)S(1)}) custom-call(s32[4]{0:T(128)S(1)} %pad_add_fusion.m, bf16[2,16,2,128,128]{4,3,2,1,0:T(8,128)(2,1)S(1)} %copy-done.3, bf16[2,16,2,128,128]{4,3,2,1,0:T(8,128)(2,1)} %collective-permute-done.5.far_ref, bf16[16,64,256]{2,1,0:T(8,128)(2,1)S(1)} %bitcast.133, ...), custom_call_target="tpu_custom_call" | custom-call | flops 536870912 | bytes 4194304 | tf_op jit(solution)/shard_map/adjoint/pallas_call | solution.py:170
  261.4 4.0 %adjoint.7 = (bf16[16,64,128]{2,1,0:T(8,128)(2,1)S(1)}, f32[16,64,128]{2,1,0:T(8,128)S(1)}) custom-call(s32[4]{0:T(128)S(1)} %pad_add_fusion.m, bf16[2,16,2,128,128]{4,3,2,1,0:T(8,128)(2,1)S(1)} %get-tuple-element.84.near_ref, bf16[2,16,2,128,128]{4,3,2,1,0:T(8,128)(2,1)} %collective-permute-done.10.far_ref, bf16[16,64,256]{2,1,0:T(8,128)(2,1)} %bitcast.52.own_ref, ...), custom_call_target="tpu_custom_call" | custom-call | flops 536870912 | bytes 4194304 | tf_op jit(solution)/shard_map/adjoint/pallas_call | solution.py:170
  266.9 7.1 %collective-permute-done.46 = bf16[16,64,128]{2,1,0:T(8,128)(2,1)S(1)} collective-permute-done((bf16[16,64,128]{2,1,0:T(8,128)(2,1)S(1)}, bf16[16,64,128]{2,1,0:T(8,128)(2,1)S(1)}, u32[]{:S(2)}, u32[]{:S(2)}) %collective-permute-start.46) | collective-permute-done | bytes 262176 | tf_op jit(solution)/shard_map/ppermute | solution.py:245
  274.0 1.9 fusion.4
  (218 shorter events, 91.1 us)
Async XLA Ops:
  0.6 5.2 %collective-permute-start.1 = (f32[16,128]{1,0:T(8,128)}, f32[16,128]{1,0:T(8,128)S(1)}, u32[]{:S(2)}, u32[]{:S(2)}) collective-permute-start(f32[16,128]{1,0:T(8,128)} %param.6), channel_id=1, source_target_pairs={{0,1},{1,0},{2,3},{3,2},{4,5},{5,4},{6,7},{7,6},{8,9},{9,8},{10,11... | collective-permute-start | bytes 24584 | tf_op jit(solution)/shard_map/ppermute | solution.py:248
  13.9 10.0 %collective-permute-start.5 = (bf16[2,16,2,128,128]{4,3,2,1,0:T(8,128)(2,1)}, bf16[2,16,2,128,128]{4,3,2,1,0:T(8,128)(2,1)}, u32[]{:S(2)}, u32[]{:S(2)}) collective-permute-start(bf16[2,16,2,128,128]{4,3,2,1,0:T(8,128)(2,1)} %get-tuple-element.83), channel_id=1, source_target_pairs={{0,8},{8,0},{16,24},{24,16},{1,9},{9,1},{17,25},{25,17},{2,10},{10... | collective-permute-start | bytes 6291464 | tf_op jit(solution)/shard_map/ppermute | solution.py:242
  13.9 18.5 %collective-permute-start.10 = (bf16[2,16,2,128,128]{4,3,2,1,0:T(8,128)(2,1)}, bf16[2,16,2,128,128]{4,3,2,1,0:T(8,128)(2,1)}, u32[]{:S(2)}, u32[]{:S(2)}) collective-permute-start(bf16[2,16,2,128,128]{4,3,2,1,0:T(8,128)(2,1)} %get-tuple-element.86), channel_id=1, source_target_pairs={{0,8},{8,0},{16,24},{24,16},{1,9},{9,1},{17,25},{25,17},{2,10},{10... | collective-permute-start | bytes 6291464 | tf_op jit(solution)/shard_map/ppermute | solution.py:242
  14.4 9.5 %collective-permute-start.6 = (bf16[16,64,128]{2,1,0:T(8,128)(2,1)}, bf16[16,64,128]{2,1,0:T(8,128)(2,1)}, u32[]{:S(2)}, u32[]{:S(2)}) collective-permute-start(bf16[16,64,128]{2,1,0:T(8,128)(2,1)} %bitcast.15), channel_id=1, source_target_pairs={{0,16},{8,24},{16,0},{24,8},{1,17},{9,25},{17,1},{25,9},{2,18},{10... | collective-permute-start | bytes 786440 | tf_op jit(solution)/shard_map/ppermute | solution.py:245
  16.1 16.3 %collective-permute-start = (bf16[16,64,128]{2,1,0:T(8,128)(2,1)}, bf16[16,64,128]{2,1,0:T(8,128)(2,1)S(1)}, u32[]{:S(2)}, u32[]{:S(2)}) collective-permute-start(bf16[16,64,128]{2,1,0:T(8,128)(2,1)} %bitcast.1), channel_id=1, source_target_pairs={{0,16},{8,24},{16,0},{24,8},{1,17},{9,25},{17,1},{25,9},{2,18},{10... | collective-permute-start | bytes 786440 | tf_op jit(solution)/shard_map/ppermute | solution.py:245
  16.5 22.0 %collective-permute-start.2 = (f32[32,128]{1,0:T(8,128)S(1)}, f32[32,128]{1,0:T(8,128)S(1)}, u32[]{:S(2)}, u32[]{:S(2)}) collective-permute-start(f32[32,128]{1,0:T(8,128)S(1)} %pad_maximum_fusion.3), channel_id=1, source_target_pairs={{0,2},{1,3},{2,0},{3,1},{4,6},{5,7},{6,4},{7,5},{8,10},{9,11},{10,... | collective-permute-start | bytes 49160 | tf_op jit(solution)/shard_map/ppermute | solution.py:248
  30.7 15.2 %collective-permute-start.7 = (bf16[16,64,256]{2,1,0:T(8,128)(2,1)}, bf16[16,64,256]{2,1,0:T(8,128)(2,1)}, u32[]{:S(2)}, u32[]{:S(2)}) collective-permute-start(bf16[16,64,256]{2,1,0:T(8,128)(2,1)} %get-tuple-element.43), channel_id=1, source_target_pairs={{0,1},{1,0},{2,3},{3,2},{4,5},{5,4},{6,7},{7,6},{8,9},{9,8},{10,11... | collective-permute-start | bytes 1572872 | tf_op jit(solution)/shard_map/ppermute | solution.py:248
  38.2 16.1 %collective-permute-start.11 = (bf16[16,64,256]{2,1,0:T(8,128)(2,1)}, bf16[16,64,256]{2,1,0:T(8,128)(2,1)}, u32[]{:S(2)}, u32[]{:S(2)}) collective-permute-start(bf16[16,64,256]{2,1,0:T(8,128)(2,1)} %get-tuple-element.49), channel_id=1, source_target_pairs={{0,1},{1,0},{2,3},{3,2},{4,5},{5,4},{6,7},{7,6},{8,9},{9,8},{10,11... | collective-permute-start | bytes 1572872 | tf_op jit(solution)/shard_map/ppermute | solution.py:248
  38.6 4.9 %collective-permute-start.3 = (f32[64,128]{1,0:T(8,128)S(1)}, f32[64,128]{1,0:T(8,128)S(1)}, u32[]{:S(2)}, u32[]{:S(2)}) collective-permute-start(f32[64,128]{1,0:T(8,128)S(1)} %pad_maximum_fusion.2), channel_id=1, source_target_pairs={{0,4},{1,5},{2,6},{3,7},{4,0},{5,1},{6,2},{7,3},{8,12},{9,13},{10,... | collective-permute-start | bytes 98312 | tf_op jit(solution)/shard_map/ppermute | solution.py:248
  48.8 12.2 %collective-permute-start.8 = (bf16[512,256]{1,0:T(8,128)(2,1)}, bf16[512,256]{1,0:T(8,128)(2,1)}, u32[]{:S(2)}, u32[]{:S(2)}) collective-permute-start(bf16[512,256]{1,0:T(8,128)(2,1)} %get-tuple-element.45), channel_id=1, source_target_pairs={{0,2},{1,3},{2,0},{3,1},{4,6},{5,7},{6,4},{7,5},{8,10},{9,11},{10,... | collective-permute-start | bytes 786440 | tf_op jit(solution)/shard_map/ppermute | solution.py:248
  57.9 7.7 %collective-permute-start.12 = (bf16[512,256]{1,0:T(8,128)(2,1)}, bf16[512,256]{1,0:T(8,128)(2,1)}, u32[]{:S(2)}, u32[]{:S(2)}) collective-permute-start(bf16[512,256]{1,0:T(8,128)(2,1)} %get-tuple-element.51), channel_id=1, source_target_pairs={{0,2},{1,3},{2,0},{3,1},{4,6},{5,7},{6,4},{7,5},{8,10},{9,11},{10,... | collective-permute-start | bytes 786440 | tf_op jit(solution)/shard_map/ppermute | solution.py:248
  59.6 1.3 collective-permute-start.4
  62.9 12.2 %collective-permute-start.9 = (bf16[256,256]{1,0:T(8,128)(2,1)S(1)}, bf16[256,256]{1,0:T(8,128)(2,1)S(1)}, u32[]{:S(2)}, u32[]{:S(2)}) collective-permute-start(bf16[256,256]{1,0:T(8,128)(2,1)S(1)} %get-tuple-element.47), channel_id=1, source_target_pairs={{0,4},{1,5},{2,6},{3,7},{4,0},{5,1},{6,2},{7,3},{8,12},{9,13},{10,... | collective-permute-start | bytes 393224 | tf_op jit(solution)/shard_map/ppermute | solution.py:248
  67.6 10.3 %collective-permute-start.13 = (bf16[256,256]{1,0:T(8,128)(2,1)S(1)}, bf16[256,256]{1,0:T(8,128)(2,1)S(1)}, u32[]{:S(2)}, u32[]{:S(2)}) collective-permute-start(bf16[256,256]{1,0:T(8,128)(2,1)S(1)} %get-tuple-element.53), channel_id=1, source_target_pairs={{0,4},{1,5},{2,6},{3,7},{4,0},{5,1},{6,2},{7,3},{8,12},{9,13},{10,... | collective-permute-start | bytes 393224 | tf_op jit(solution)/shard_map/ppermute | solution.py:248
  75.2 10.2 %collective-permute-start.19 = (bf16[256,256]{1,0:T(8,128)(2,1)S(1)}, bf16[256,256]{1,0:T(8,128)(2,1)S(1)}, u32[]{:S(2)}, u32[]{:S(2)}) collective-permute-start(bf16[256,256]{1,0:T(8,128)(2,1)S(1)} %fusion.11.own_ref), channel_id=1, source_target_pairs={{0,4},{1,5},{2,6},{3,7},{4,0},{5,1},{6,2},{7,3},{8,12},{9,13},{10,... | collective-permute-start | bytes 393224 | tf_op jit(solution)/shard_map/ppermute | solution.py:248
  77.9 11.0 %collective-permute-start.23 = (bf16[256,256]{1,0:T(8,128)(2,1)S(1)}, bf16[256,256]{1,0:T(8,128)(2,1)S(1)}, u32[]{:S(2)}, u32[]{:S(2)}) collective-permute-start(bf16[256,256]{1,0:T(8,128)(2,1)S(1)} %fusion.13.own_ref), channel_id=1, source_target_pairs={{0,4},{1,5},{2,6},{3,7},{4,0},{5,1},{6,2},{7,3},{8,12},{9,13},{10,... | collective-permute-start | bytes 393224 | tf_op jit(solution)/shard_map/ppermute | solution.py:248
  86.6 11.6 %collective-permute-start.20 = (bf16[512,256]{1,0:T(8,128)(2,1)}, bf16[512,256]{1,0:T(8,128)(2,1)}, u32[]{:S(2)}, u32[]{:S(2)}) collective-permute-start(bf16[512,256]{1,0:T(8,128)(2,1)} %join.8.own_ref), channel_id=1, source_target_pairs={{0,2},{1,3},{2,0},{3,1},{4,6},{5,7},{6,4},{7,5},{8,10},{9,11},{10,... | collective-permute-start | bytes 786440 | tf_op jit(solution)/shard_map/ppermute | solution.py:248
  90.2 10.6 %collective-permute-start.24 = (bf16[512,256]{1,0:T(8,128)(2,1)}, bf16[512,256]{1,0:T(8,128)(2,1)}, u32[]{:S(2)}, u32[]{:S(2)}) collective-permute-start(bf16[512,256]{1,0:T(8,128)(2,1)} %join.10.own_ref), channel_id=1, source_target_pairs={{0,2},{1,3},{2,0},{3,1},{4,6},{5,7},{6,4},{7,5},{8,10},{9,11},{10,... | collective-permute-start | bytes 786440 | tf_op jit(solution)/shard_map/ppermute | solution.py:248
  99.3 14.9 %collective-permute-start.21 = (bf16[16,64,256]{2,1,0:T(8,128)(2,1)S(1)}, bf16[16,64,256]{2,1,0:T(8,128)(2,1)S(1)}, u32[]{:S(2)}, u32[]{:S(2)}) collective-permute-start(bf16[16,64,256]{2,1,0:T(8,128)(2,1)S(1)} %bitcast.128), channel_id=1, source_target_pairs={{0,1},{1,0},{2,3},{3,2},{4,5},{5,4},{6,7},{7,6},{8,9},{9,8},{10,11... | collective-permute-start | bytes 1572872 | tf_op jit(solution)/shard_map/ppermute | solution.py:248
  101.9 19.9 %collective-permute-start.25 = (bf16[16,64,256]{2,1,0:T(8,128)(2,1)S(1)}, bf16[16,64,256]{2,1,0:T(8,128)(2,1)S(1)}, u32[]{:S(2)}, u32[]{:S(2)}) collective-permute-start(bf16[16,64,256]{2,1,0:T(8,128)(2,1)S(1)} %bitcast.130), channel_id=1, source_target_pairs={{0,1},{1,0},{2,3},{3,2},{4,5},{5,4},{6,7},{7,6},{8,9},{9,8},{10,11... | collective-permute-start | bytes 1572872 | tf_op jit(solution)/shard_map/ppermute | solution.py:248
  102.6 25.3 %collective-permute-start.14 = (f32[16,128]{1,0:T(8,128)S(1)}, f32[16,128]{1,0:T(8,128)S(1)}, u32[]{:S(2)}, u32[]{:S(2)}) collective-permute-start(f32[16,128]{1,0:T(8,128)S(1)} %pad_maximum_fusion.5), channel_id=1, source_target_pairs={{0,1},{1,0},{2,3},{3,2},{4,5},{5,4},{6,7},{7,6},{8,9},{9,8},{10,11... | collective-permute-start | bytes 24584 | tf_op jit(solution)/shard_map/ppermute | solution.py:248
  118.8 25.6 %collective-permute-start.22 = (bf16[2,16,64,128]{3,2,1,0:T(8,128)(2,1)}, bf16[2,16,64,128]{3,2,1,0:T(8,128)(2,1)}, u32[]{:S(2)}, u32[]{:S(2)}) collective-permute-start(bf16[2,16,64,128]{3,2,1,0:T(8,128)(2,1)} %adjoint.4.one_ref), channel_id=1, source_target_pairs={{0,16},{8,24},{16,0},{24,8},{1,17},{9,25},{17,1},{25,9},{2,18},{10... | collective-permute-start | bytes 1572872 | tf_op jit(solution)/shard_map/ppermute | solution.py:245
  126.4 26.3 %collective-permute-start.26 = (bf16[2,16,64,128]{3,2,1,0:T(8,128)(2,1)}, bf16[2,16,64,128]{3,2,1,0:T(8,128)(2,1)}, u32[]{:S(2)}, u32[]{:S(2)}) collective-permute-start(bf16[2,16,64,128]{3,2,1,0:T(8,128)(2,1)} %adjoint.5.one_ref), channel_id=1, source_target_pairs={{0,16},{8,24},{16,0},{24,8},{1,17},{9,25},{17,1},{25,9},{2,18},{10... | collective-permute-start | bytes 1572872 | tf_op jit(solution)/shard_map/ppermute | solution.py:245
  127.9 3.7 %collective-permute-start.15 = (f32[16,128]{1,0:T(8,128)S(1)}, f32[16,128]{1,0:T(8,128)S(1)}, u32[]{:S(2)}, u32[]{:S(2)}) collective-permute-start(f32[16,128]{1,0:T(8,128)S(1)} %fusion.19), channel_id=1, source_target_pairs={{0,2},{1,3},{2,0},{3,1},{4,6},{5,7},{6,4},{7,5},{8,10},{9,11},{10,... | collective-permute-start | bytes 24584 | tf_op jit(solution)/shard_map/ppermute | solution.py:248
  131.6 4.6 %collective-permute-start.16 = (f32[16,128]{1,0:T(8,128)S(1)}, f32[16,128]{1,0:T(8,128)S(1)}, u32[]{:S(2)}, u32[]{:S(2)}) collective-permute-start(f32[16,128]{1,0:T(8,128)S(1)} %add.201), channel_id=1, source_target_pairs={{0,4},{1,5},{2,6},{3,7},{4,0},{5,1},{6,2},{7,3},{8,12},{9,13},{10,... | collective-permute-start | bytes 24584 | tf_op jit(solution)/shard_map/ppermute | solution.py:248
  136.2 3.7 %collective-permute-start.17 = (f32[16,128]{1,0:T(8,128)S(1)}, f32[16,128]{1,0:T(8,128)S(1)}, u32[]{:S(2)}, u32[]{:S(2)}) collective-permute-start(f32[16,128]{1,0:T(8,128)S(1)} %add.202), channel_id=1, source_target_pairs={{0,16},{8,24},{16,0},{24,8},{1,17},{9,25},{17,1},{25,9},{2,18},{10... | collective-permute-start | bytes 24584 | tf_op jit(solution)/shard_map/ppermute | solution.py:245
  139.8 1.2 collective-permute-start.18
  151.2 15.1 %collective-permute-start.28 = (bf16[16,64,256]{2,1,0:T(8,128)(2,1)}, bf16[16,64,256]{2,1,0:T(8,128)(2,1)}, u32[]{:S(2)}, u32[]{:S(2)}) collective-permute-start(bf16[16,64,256]{2,1,0:T(8,128)(2,1)} %get-tuple-element.58), channel_id=1, source_target_pairs={{0,1},{1,0},{2,3},{3,2},{4,5},{5,4},{6,7},{7,6},{8,9},{9,8},{10,11... | collective-permute-start | bytes 1572872 | tf_op jit(solution)/shard_map/ppermute | solution.py:248
  158.6 18.1 %collective-permute-start.31 = (bf16[16,64,256]{2,1,0:T(8,128)(2,1)}, bf16[16,64,256]{2,1,0:T(8,128)(2,1)}, u32[]{:S(2)}, u32[]{:S(2)}) collective-permute-start(bf16[16,64,256]{2,1,0:T(8,128)(2,1)} %get-tuple-element.64), channel_id=1, source_target_pairs={{0,1},{1,0},{2,3},{3,2},{4,5},{5,4},{6,7},{7,6},{8,9},{9,8},{10,11... | collective-permute-start | bytes 1572872 | tf_op jit(solution)/shard_map/ppermute | solution.py:248
  159.2 3.5 %collective-permute-start.27 = (f32[32]{0:T(128)S(1)}, f32[32]{0:T(128)}, u32[]{:S(2)}, u32[]{:S(2)}) collective-permute-start(f32[32]{0:T(128)S(1)} %copy-done.32), channel_id=1, source_target_pairs={{0,16},{8,24},{16,0},{24,8},{1,17},{9,25},{17,1},{25,9},{2,18},{10... | collective-permute-start | bytes 392 | tf_op jit(solution)/shard_map/ppermute | solution.py:245
  169.8 20.8 %collective-permute-start.29 = (bf16[512,256]{1,0:T(8,128)(2,1)}, bf16[512,256]{1,0:T(8,128)(2,1)}, u32[]{:S(2)}, u32[]{:S(2)}) collective-permute-start(bf16[512,256]{1,0:T(8,128)(2,1)} %get-tuple-element.60), channel_id=1, source_target_pairs={{0,2},{1,3},{2,0},{3,1},{4,6},{5,7},{6,4},{7,5},{8,10},{9,11},{10,... | collective-permute-start | bytes 786440 | tf_op jit(solution)/shard_map/ppermute | solution.py:248
  179.2 15.3 %collective-permute-start.32 = (bf16[512,256]{1,0:T(8,128)(2,1)}, bf16[512,256]{1,0:T(8,128)(2,1)}, u32[]{:S(2)}, u32[]{:S(2)}) collective-permute-start(bf16[512,256]{1,0:T(8,128)(2,1)} %get-tuple-element.66), channel_id=1, source_target_pairs={{0,2},{1,3},{2,0},{3,1},{4,6},{5,7},{6,4},{7,5},{8,10},{9,11},{10,... | collective-permute-start | bytes 786440 | tf_op jit(solution)/shard_map/ppermute | solution.py:248
  191.7 11.3 %collective-permute-start.30 = (bf16[256,256]{1,0:T(8,128)(2,1)S(1)}, bf16[256,256]{1,0:T(8,128)(2,1)S(1)}, u32[]{:S(2)}, u32[]{:S(2)}) collective-permute-start(bf16[256,256]{1,0:T(8,128)(2,1)S(1)} %get-tuple-element.62), channel_id=1, source_target_pairs={{0,4},{1,5},{2,6},{3,7},{4,0},{5,1},{6,2},{7,3},{8,12},{9,13},{10,... | collective-permute-start | bytes 393224 | tf_op jit(solution)/shard_map/ppermute | solution.py:248
  195.6 11.4 %collective-permute-start.33 = (bf16[256,256]{1,0:T(8,128)(2,1)S(1)}, bf16[256,256]{1,0:T(8,128)(2,1)S(1)}, u32[]{:S(2)}, u32[]{:S(2)}) collective-permute-start(bf16[256,256]{1,0:T(8,128)(2,1)S(1)} %get-tuple-element.68), channel_id=1, source_target_pairs={{0,4},{1,5},{2,6},{3,7},{4,0},{5,1},{6,2},{7,3},{8,12},{9,13},{10,... | collective-permute-start | bytes 393224 | tf_op jit(solution)/shard_map/ppermute | solution.py:248
  203.1 10.2 %collective-permute-start.42 = (bf16[256,256]{1,0:T(8,128)(2,1)S(1)}, bf16[256,256]{1,0:T(8,128)(2,1)S(1)}, u32[]{:S(2)}, u32[]{:S(2)}) collective-permute-start(bf16[256,256]{1,0:T(8,128)(2,1)S(1)} %fusion.12.own_ref), channel_id=1, source_target_pairs={{0,4},{1,5},{2,6},{3,7},{4,0},{5,1},{6,2},{7,3},{8,12},{9,13},{10,... | collective-permute-start | bytes 393224 | tf_op jit(solution)/shard_map/ppermute | solution.py:248
  207.1 9.0 %collective-permute-start.39 = (bf16[256,256]{1,0:T(8,128)(2,1)S(1)}, bf16[256,256]{1,0:T(8,128)(2,1)S(1)}, u32[]{:S(2)}, u32[]{:S(2)}) collective-permute-start(bf16[256,256]{1,0:T(8,128)(2,1)S(1)} %fusion.14.own_ref), channel_id=1, source_target_pairs={{0,4},{1,5},{2,6},{3,7},{4,0},{5,1},{6,2},{7,3},{8,12},{9,13},{10,... | collective-permute-start | bytes 393224 | tf_op jit(solution)/shard_map/ppermute | solution.py:248
  207.4 43.2 %copy-start.3 = (bf16[2,16,2,128,128]{4,3,2,1,0:T(8,128)(2,1)S(1)}, bf16[2,16,2,128,128]{4,3,2,1,0:T(8,128)(2,1)}, u32[]{:S(2)}) copy-start(bf16[2,16,2,128,128]{4,3,2,1,0:T(8,128)(2,1)} %get-tuple-element.85.near_ref) | copy-start | bytes 6291460
  213.9 9.4 %collective-permute-start.43 = (bf16[512,256]{1,0:T(8,128)(2,1)S(1)}, bf16[512,256]{1,0:T(8,128)(2,1)S(1)}, u32[]{:S(2)}, u32[]{:S(2)}) collective-permute-start(bf16[512,256]{1,0:T(8,128)(2,1)S(1)} %join.14.own_ref), channel_id=1, source_target_pairs={{0,2},{1,3},{2,0},{3,1},{4,6},{5,7},{6,4},{7,5},{8,10},{9,11},{10,... | collective-permute-start | bytes 786440 | tf_op jit(solution)/shard_map/ppermute | solution.py:248
  216.7 10.0 %collective-permute-start.40 = (bf16[512,256]{1,0:T(8,128)(2,1)S(1)}, bf16[512,256]{1,0:T(8,128)(2,1)S(1)}, u32[]{:S(2)}, u32[]{:S(2)}) collective-permute-start(bf16[512,256]{1,0:T(8,128)(2,1)S(1)} %join.12.own_ref), channel_id=1, source_target_pairs={{0,2},{1,3},{2,0},{3,1},{4,6},{5,7},{6,4},{7,5},{8,10},{9,11},{10,... | collective-permute-start | bytes 786440 | tf_op jit(solution)/shard_map/ppermute | solution.py:248
  223.9 26.6 %collective-permute-start.44 = (bf16[16,64,256]{2,1,0:T(8,128)(2,1)S(1)}, bf16[16,64,256]{2,1,0:T(8,128)(2,1)S(1)}, u32[]{:S(2)}, u32[]{:S(2)}) collective-permute-start(bf16[16,64,256]{2,1,0:T(8,128)(2,1)S(1)} %bitcast.132), channel_id=1, source_target_pairs={{0,1},{1,0},{2,3},{3,2},{4,5},{5,4},{6,7},{7,6},{8,9},{9,8},{10,11... | collective-permute-start | bytes 1572872 | tf_op jit(solution)/shard_map/ppermute | solution.py:248
  225.5 13.0 %collective-permute-start.34 = (f32[24,128]{1,0:T(8,128)S(1)}, f32[24,128]{1,0:T(8,128)S(1)}, u32[]{:S(2)}, u32[]{:S(2)}) collective-permute-start(f32[24,128]{1,0:T(8,128)S(1)} %pad_maximum_fusion.4), channel_id=1, source_target_pairs={{0,1},{1,0},{2,3},{3,2},{4,5},{5,4},{6,7},{7,6},{8,9},{9,8},{10,11... | collective-permute-start | bytes 36872 | tf_op jit(solution)/shard_map/ppermute | solution.py:248
  228.0 33.4 %collective-permute-start.41 = (bf16[16,64,256]{2,1,0:T(8,128)(2,1)}, bf16[16,64,256]{2,1,0:T(8,128)(2,1)}, u32[]{:S(2)}, u32[]{:S(2)}) collective-permute-start(bf16[16,64,256]{2,1,0:T(8,128)(2,1)} %bitcast.52.own_ref), channel_id=1, source_target_pairs={{0,1},{1,0},{2,3},{3,2},{4,5},{5,4},{6,7},{7,6},{8,9},{9,8},{10,11... | collective-permute-start | bytes 1572872 | tf_op jit(solution)/shard_map/ppermute | solution.py:248
  238.5 3.7 %collective-permute-start.35 = (f32[24,128]{1,0:T(8,128)S(1)}, f32[24,128]{1,0:T(8,128)S(1)}, u32[]{:S(2)}, u32[]{:S(2)}) collective-permute-start(f32[24,128]{1,0:T(8,128)S(1)} %fusion.20), channel_id=1, source_target_pairs={{0,2},{1,3},{2,0},{3,1},{4,6},{5,7},{6,4},{7,5},{8,10},{9,11},{10,... | collective-permute-start | bytes 36872 | tf_op jit(solution)/shard_map/ppermute | solution.py:248
  242.2 4.6 %collective-permute-start.36 = (f32[24,128]{1,0:T(8,128)S(1)}, f32[24,128]{1,0:T(8,128)S(1)}, u32[]{:S(2)}, u32[]{:S(2)}) collective-permute-start(f32[24,128]{1,0:T(8,128)S(1)} %add.217), channel_id=1, source_target_pairs={{0,4},{1,5},{2,6},{3,7},{4,0},{5,1},{6,2},{7,3},{8,12},{9,13},{10,... | collective-permute-start | bytes 36872 | tf_op jit(solution)/shard_map/ppermute | solution.py:248
  246.8 3.7 %collective-permute-start.37 = (f32[24,128]{1,0:T(8,128)S(1)}, f32[24,128]{1,0:T(8,128)S(1)}, u32[]{:S(2)}, u32[]{:S(2)}) collective-permute-start(f32[24,128]{1,0:T(8,128)S(1)} %add.218), channel_id=1, source_target_pairs={{0,16},{8,24},{16,0},{24,8},{1,17},{9,25},{17,1},{25,9},{2,18},{10... | collective-permute-start | bytes 36872 | tf_op jit(solution)/shard_map/ppermute | solution.py:245
  250.5 6.2 %collective-permute-start.38 = (f32[24,128]{1,0:T(8,128)S(1)}, f32[24,128]{1,0:T(8,128)S(1)}, u32[]{:S(2)}, u32[]{:S(2)}) collective-permute-start(f32[24,128]{1,0:T(8,128)S(1)} %add.219), channel_id=1, source_target_pairs={{0,8},{8,0},{16,24},{24,16},{1,9},{9,1},{17,25},{25,17},{2,10},{10... | collective-permute-start | bytes 36872 | tf_op jit(solution)/shard_map/ppermute | solution.py:242
  255.0 10.8 %collective-permute-start.45 = (bf16[16,64,128]{2,1,0:T(8,128)(2,1)S(1)}, bf16[16,64,128]{2,1,0:T(8,128)(2,1)}, u32[]{:S(2)}, u32[]{:S(2)}) collective-permute-start(bf16[16,64,128]{2,1,0:T(8,128)(2,1)S(1)} %get-tuple-element.71), channel_id=1, source_target_pairs={{0,16},{8,24},{16,0},{24,8},{1,17},{9,25},{17,1},{25,9},{2,18},{10... | collective-permute-start | bytes 786440 | tf_op jit(solution)/shard_map/ppermute | solution.py:245
  265.4 8.5 %collective-permute-start.46 = (bf16[16,64,128]{2,1,0:T(8,128)(2,1)S(1)}, bf16[16,64,128]{2,1,0:T(8,128)(2,1)S(1)}, u32[]{:S(2)}, u32[]{:S(2)}) collective-permute-start(bf16[16,64,128]{2,1,0:T(8,128)(2,1)S(1)} %get-tuple-element.75), channel_id=1, source_target_pairs={{0,16},{8,24},{16,0},{24,8},{1,17},{9,25},{17,1},{25,9},{2,18},{10... | collective-permute-start | bytes 786440 | tf_op jit(solution)/shard_map/ppermute | solution.py:245
  (38 other events, 282.5 us)

commit v2 on v0

--- a/solution.py
+++ b/solution.py
@@ -11,6 +11,7 @@
 KERNEL_BYTES = 16 * 2 ** 20
 F32 = jnp.float32
 BF16 = jnp.bfloat16
+ANYWHERE = pl.BlockSpec(memory_space=pl.ANY)
 NT = (((1,), (1,)), ((), ()))
 NN = (((1,), (0,)), ((), ()))
 
@@ -70,11 +71,12 @@
     )
 
 
-def forward_call(plan, chunk, meta, near, far, first, vectors):
+def forward_call(plan, chunk, meta, near, far, first, vectors, wait=()):
     blk_of = lambda p, m: 1 - (m[2] ^ p)
     step, steps = plan.step, plan.steps
 
-    def kernel(m, near_ref, far_ref, one_ref, two_ref, send_ref, keep_ref):
+    def kernel(m, near_ref, far_ref, one_ref, two_ref, *refs):
+        send_ref, keep_ref = refs[len(wait):]
         phase = pl.program_id(0)
         blk = blk_of(phase, m)
 
@@ -118,24 +120,25 @@
         grid_spec=pltpu.PrefetchScalarGridSpec(
             num_scalar_prefetch=1,
             grid=(2, steps),
-            in_specs=[part_spec(plan, blk_of)] * 2 + vec_specs,
+            in_specs=[part_spec(plan, blk_of)] * 2 + vec_specs + [ANYWHERE] * len(wait),
             out_specs=[
                 pl.BlockSpec(out, lambda p, t, m: (jnp.where(p == 0, t, steps - 1), 0, 0)),
                 pl.BlockSpec(out, lambda p, t, m: (jnp.where(p == 0, 0, t), 0, 0)),
             ],
         ),
-        out_shape=[jax.ShapeDtypeStruct(shape, BF16), jax.ShapeDtypeStruct(shape, F32)],
+        out_shape=[jax.ShapeDtypeStruct(shape, BF16)] * 2,
         cost_estimate=cost(plan.flops, 16 * plan.part * plan.sensors * plan.sources),
         compiler_params=pltpu.CompilerParams(vmem_limit_bytes=KERNEL_BYTES),
         name="forward",
-    )(meta, near, far, *vectors)
-
-
-def adjoint_call(plan, meta, near, far, halves, last):
+    )(meta, near, far, *vectors, *wait)
+
+
+def adjoint_call(plan, meta, near, far, halves, last, wait=()):
     blk_of = lambda p, m: 1 - p
     step, steps = plan.step, plan.steps
 
     def kernel(m, near_ref, far_ref, own_ref, got_ref, *outs):
+        outs = outs[len(wait):]
         phase = pl.program_id(0)
         mine = blk_of(phase, m) == m[2]
 
@@ -177,14 +180,14 @@
                 part_spec(plan, blk_of),
                 pl.BlockSpec(size, lambda p, t, m: (t, 0, 0)),
                 pl.BlockSpec(size, lambda p, t, m: (t, 0, 0)),
-            ],
+            ] + [ANYWHERE] * len(wait),
             out_specs=out_specs,
         ),
         out_shape=out_shape,
         cost_estimate=cost(plan.flops, 16 * plan.part * plan.sensors * plan.sources),
         compiler_params=pltpu.CompilerParams(vmem_limit_bytes=KERNEL_BYTES),
         name="adjoint",
-    )(meta, near, far, *halves)
+    )(meta, near, far, *halves, *wait)
 
 
 def split_call(plan, meta, keep, got):
@@ -194,7 +197,7 @@
     def kernel(m, keep_ref, got_ref, mine_ref, *sends):
         for d in range(groups):
             place = pl.ds(pl.multiple_of((m[3] ^ d) * piece, piece), piece)
-            total = keep_ref[place] + got_ref[place].astype(F32)
+            total = keep_ref[place].astype(F32) + got_ref[place].astype(F32)
             if d == 0:
                 mine_ref[...] = total
             else:
@@ -235,13 +238,152 @@
     return out.reshape(plan.part, plan.rows, width)
 
 
+def ordered(array, *earlier):
+    def kernel(*refs):
+        del refs
+
+    return pl.pallas_call(
+        kernel,
+        in_specs=[ANYWHERE] * (1 + len(earlier)),
+        out_specs=ANYWHERE,
+        out_shape=jax.ShapeDtypeStruct(array.shape, array.dtype),
+        input_output_aliases={0: 0},
+        cost_estimate=cost(0, 0),
+        compiler_params=pltpu.CompilerParams(vmem_limit_bytes=KERNEL_BYTES),
+        name="ordered",
+    )(array, *earlier)
+
+
+def lanes(array):
+    total = jnp.sum(array.reshape(-1, 8, array.shape[-1]), axis=0)
+    return sum(total[:, i:i + 128] for i in range(0, array.shape[-1], 128))
+
+
+def sensor_call(plan, chunk, meta, weights, pieces, alpha=None, damping=None, old=None):
+    piece, rows, groups = plan.piece, plan.rows, plan.groups
+    width = pieces[0].shape[-1]
+    count = max(1, piece // rows)
+    high = piece // count
+    second = old is not None
+
+    def kernel(m, *refs):
+        if second:
+            alpha_ref, damp_ref, old_ref, *refs = refs
+        weights_ref, *refs = refs
+        ins, (out_ref, *more) = refs[:groups], refs[groups:]
+        stats_ref = more[-1]
+        square = cross = jnp.zeros((8, 128), F32)
+        for c in range(count):
+            at = pl.ds(c * high, high)
+            freq = chunk * plan.part + (m[3] * piece + c * high) // rows
+            field = ins[0][at]
+            for ref in ins[1:]:
+                field = field + ref[at].astype(F32)
+            if second:
+                factor = 1.0 - alpha_ref[0] * damp_ref[freq]
+                field = factor * old_ref[at] - alpha_ref[0] * field
+            scaled = weights_ref[pl.ds(freq, 1)] * field
+            out_ref[at] = scaled.astype(BF16)
+            square = square + lanes(scaled * field)
+            if second:
+                cross = cross + lanes(scaled * old_ref[at])
+            else:
+                more[0][at] = field
+        stats_ref[0:8] = square
+        stats_ref[8:16] = cross
+
+    whole = pl.BlockSpec(memory_space=pltpu.VMEM)
+    scalars = pl.BlockSpec(memory_space=pltpu.SMEM)
+    first_out = [] if second else [jax.ShapeDtypeStruct((piece, width), F32)]
+    extra = (alpha, damping, old) if second else ()
+    out_shape = [jax.ShapeDtypeStruct((piece, width), BF16)] + first_out
+    out_shape = out_shape + [jax.ShapeDtypeStruct((16, 128), F32)]
+    return pl.pallas_call(
+        kernel,
+        in_specs=[scalars] + ([scalars] * 2 + [whole] if second else []) + [whole] * (1 + groups),
+        out_specs=[whole] * len(out_shape),
+        out_shape=out_shape,
+        cost_estimate=cost(8 * piece * width, 16 * piece * width),
+        compiler_params=pltpu.CompilerParams(vmem_limit_bytes=KERNEL_BYTES),
+        name="sensor",
+    )(meta, *extra, weights, *pieces)
+
+
+def norms_call(plan, damping, start):
+    def kernel(damp_ref, start_ref, stats_ref):
+        plain = damped = jnp.zeros((8, 128), F32)
+        for f in range(plan.block):
+            term = lanes(start_ref[f] * start_ref[f])
+            plain = plain + term
+            damped = damped + damp_ref[f] * term
+        stats_ref[0:8] = plain
+        stats_ref[8:16] = damped
+
+    whole = pl.BlockSpec(memory_space=pltpu.VMEM)
+    return pl.pallas_call(
+        kernel,
+        in_specs=[pl.BlockSpec(memory_space=pltpu.SMEM), whole],
+        out_specs=whole,
+        out_shape=jax.ShapeDtypeStruct((16, 128), F32),
+        cost_estimate=cost(2 * start.size, 4 * start.size),
+        compiler_params=pltpu.CompilerParams(vmem_limit_bytes=KERNEL_BYTES),
+        name="norms",
+    )(damping, start)
+
+
+def residual_call(plan, chunk, alpha, damping, start, mine, got):
+    part, rows, sources = plan.part, plan.rows, plan.sources
+
+    def kernel(alpha_ref, damp_ref, start_ref, mine_ref, got_ref, image_ref, out_ref, stats_ref):
+        plain = damped = mixed = jnp.zeros((8, 128), F32)
+        for f in range(part):
+            damp = damp_ref[chunk * part + f]
+            begin = start_ref[f]
+            image = mine_ref[f].astype(F32) + got_ref[f].astype(F32) + damp * begin
+            residual = begin - alpha_ref[0] * image
+            image_ref[f] = image
+            out_ref[f] = residual
+            term = lanes(residual * residual)
+            plain = plain + term
+            damped = damped + damp * term
+            mixed = mixed + damp * lanes(residual * begin)
+        stats_ref[0:8] = plain
+        stats_ref[8:16] = damped
+        stats_ref[16:24] = mixed
+
+    block = (part, rows, sources)
+    scalars = pl.BlockSpec(memory_space=pltpu.SMEM)
+    out = jax.ShapeDtypeStruct(block, F32)
+    return pl.pallas_call(
+        kernel,
+        grid=(1,),
+        in_specs=[
+            scalars,
+            scalars,
+            pl.BlockSpec(block, lambda i: (chunk, 0, 0)),
+            pl.BlockSpec((None,) + block, lambda i: (0, 0, 0, 0)),
+            pl.BlockSpec((None,) + block, lambda i: (1, 0, 0, 0)),
+        ],
+        out_specs=[
+            pl.BlockSpec(block, lambda i: (0, 0, 0)),
+            pl.BlockSpec(block, lambda i: (0, 0, 0)),
+            pl.BlockSpec((24, 128), lambda i: (0, 0)),
+        ],
+        out_shape=[out, out, jax.ShapeDtypeStruct((24, 128), F32)],
+        cost_estimate=cost(8 * part * rows * sources, 16 * part * rows * sources),
+        compiler_params=pltpu.CompilerParams(vmem_limit_bytes=KERNEL_BYTES),
+        name="residual",
+    )(alpha, damping, start, mine, got)
+
+
 def body(n_sens, n_src, operator, right_side, noise_weights, damping):
     plan = Plan(operator, right_side, n_sens, n_src, CHUNKS)
     sens, src = lax.axis_index("sens"), lax.axis_index("src")
-    pair, core = sens // 2, sens % 2
-    half, group = src % 2, src // 2
+    pair, core, half, group = sens // 2, sens % 2, src % 2, src // 2
     meta = jnp.stack([pair, core, half, group]).astype(jnp.int32)
     part, rows, block = plan.part, plan.rows, plan.block
+    levels = range(n_src.bit_length() - 1)
+    chunks = range(plan.chunks)
 
     def to_core(array):
         return lax.ppermute(array, "sens", [(i, i ^ 1) for i in range(n_sens)])
@@ -249,118 +391,112 @@
     def to_pair(array):
         return lax.ppermute(array, "sens", [(i, i ^ 2) for i in range(n_sens)])
 
-    def to_half(array):
-        return lax.ppermute(array, "src", [(j, j ^ 1) for j in range(n_src)])
-
-    def to_group(array, d):
-        return lax.ppermute(array, "src", [(j, j ^ (2 * d)) for j in range(n_src)])
-
-    def src_bits():
-        return [2 ** bit for bit in range(n_src.bit_length() - 1)]
-
-    def total(values):
-        sums = jnp.zeros((1, 128), F32).at[0, : len(values)].set(jnp.stack(values))
-        sums = sums + to_core(sums)
-        for bit in src_bits():
-            sums = sums + lax.ppermute(sums, "src", [(j, j ^ bit) for j in range(n_src)])
-        return (sums + to_pair(sums))[0]
-
-    def all_weights(table):
-        for bit in src_bits():
-            other = lax.ppermute(table, "src", [(j, j ^ bit) for j in range(n_src)])
-            low = (src // bit) % 2 == 0
-            table = jnp.concatenate(
-                [jnp.where(low, table, other), jnp.where(low, other, table)], axis=0
-            )
-        return table
+    def to_src(array, step):
+        return lax.ppermute(array, "src", [(j, j ^ step) for j in range(n_src)])
+
+    def in_turn(arrays, move):
+        moved = []
+        for k, array in enumerate(arrays):
+            if k > 0:
+                array = arrays[k] = ordered(array, moved[-1])
+            moved.append(move(array))
+        return moved
+
+    def total(sums):
+        steps = [sums]
+        for level in levels:
+            steps.append(steps[-1] + to_src(steps[-1], 1 << level))
+        steps.append(steps[-1] + to_pair(steps[-1]))
+        steps.append(steps[-1] + to_core(steps[-1]))
+        return jnp.sum(steps[-1].reshape(-1, 8 * 128), axis=1), steps
+
+    def double(table, level):
+        other = to_src(table, 1 << level)
+        low = (src >> level) % 2 == 0
+        return jnp.concatenate([jnp.where(low, table, other), jnp.where(low, other, table)], axis=0)
 
     whole = operator.reshape(plan.pairs, 2, block, 2, plan.sensors, plan.sources)
     start = right_side.reshape(block, rows, plan.sources)
-    chunks = range(plan.chunks)
-
-    sent_b = [start[k * part:(k + 1) * part].astype(BF16) for k in chunks]
-    got_b = [to_pair(sent) for sent in sent_b]
-    core, *_ = lax.optimization_barrier((core, *sent_b))
 
     def half_of(k, which):
         size = (plan.pairs, 1, part, 2, plan.sensors, plan.sources)
         cut = lax.dynamic_slice(whole, (0, which, k * part, 0, 0, 0), size)
         return cut.reshape(plan.pairs, part, 2, plan.sensors, plan.sources)
 
-    near, far = [], []
-    for k in chunks:
-        far.append(to_core(half_of(k, 1 - core)))
-        near.append(half_of(k, core))
-
-    weights = all_weights(noise_weights)
+    sent_b = [start[k * part:(k + 1) * part].astype(BF16) for k in chunks]
+    got_b = [to_pair(sent) for sent in sent_b]
+    now = ordered(meta, *sent_b)[1]
+    weights = double(noise_weights, 0)
+
+    for level in levels[1:]:
+        weights = double(weights, level)
     weights = weights.reshape(plan.pairs, 2, block, plan.sensors)
     weights_near = lax.dynamic_index_in_dim(weights, core, 1, keepdims=False)
     weights_far = to_core(lax.dynamic_index_in_dim(weights, 1 - core, 1, keepdims=False))
     weights = jnp.concatenate([weights_near, weights_far], axis=-1)
     weights = lax.dynamic_index_in_dim(weights, pair ^ half, 0, keepdims=False)
     damping_row = jnp.where(half == 0, damping, to_pair(damping))
-    count = max(1, plan.piece // rows)
-
-    def piece_of(k, table):
-        place = k * part + group * plan.piece // rows
-        cut = lax.dynamic_slice_in_dim(table, place, count, 0)
-        return cut.reshape(count, 1, -1)
-
-    def reduce_field(send, keep):
-        mine, *sends = split_call(plan, meta, keep, to_half(send))
-        for d, piece in enumerate(sends):
-            mine = mine + to_group(piece, d + 1).astype(F32)
-        return mine.reshape(count, plan.piece // count, -1)
+    steps = [2 * d for d in range(1, plan.groups)]
+
+    def reduce_field(keep, got):
+        mine, *sends = split_call(plan, meta, keep, got)
+        return [mine] + [to_src(piece, step) for piece, step in zip(sends, steps)]
 
     def gather_field(weighted):
-        weighted = weighted.astype(BF16).reshape(plan.piece, -1)
-        pieces = [weighted] + [to_group(weighted, d) for d in range(1, plan.groups)]
-        own = place_call(plan, meta, pieces)
-        return own, to_half(own)
-
-    field, products = [], []
+        return place_call(plan, meta, [weighted] + [to_src(weighted, step) for step in steps])
+
+    def to_half(array):
+        return to_src(array, 1)
+
+    near, far, pairs = [], [], []
     for k in chunks:
-        send, keep = forward_call(plan, k, meta, near[k], far[k], True, (start, got_b[k]))
-        field.append(reduce_field(send, keep))
-    scaled = [piece_of(k, weights) * field[k] for k in chunks]
+        far.append(to_core(half_of(k, 1 - now)))
+        near.append(half_of(k, now))
+        pairs.append(forward_call(plan, k, meta, near[k], far[k], True, (start, got_b[k])))
+        now = ordered(meta, pairs[k][0])[1]
+    got = in_turn([send for send, _ in pairs], to_half)
+    pieces = [reduce_field(pairs[k][1], got[k]) for k in chunks]
+    scaled, field, stats = zip(*[sensor_call(plan, k, meta, weights, pieces[k]) for k in chunks])
+    norms = norms_call(plan, damping, start)
+    sums, steps_0 = total(norms + jnp.pad(sum(one[0:8] for one in stats), ((8, 0), (0, 0))))
+    norm_0, curve_0 = sums[0], sums[1]
+    alpha_0 = (norm_0 / curve_0)[None]
+
+    own = [gather_field(scaled[k]) for k in chunks]
+    got = in_turn(own, to_half)
+    back = []
     for k in chunks:
-        back = adjoint_call(plan, meta, near[k], far[k], gather_field(scaled[k]), False)
-        products.append((back, to_pair(back)))
-    damp = damping[:, None, None]
-    norm, curve = jnp.sum(start * start), jnp.sum(damp * start * start)
-    for k in chunks:
-        curve = curve + jnp.sum(scaled[k] * field[k])
-    sums = total([norm, curve])
-    norm_0, curve_0 = sums[0], sums[1]
-    alpha_0 = norm_0 / curve_0
-
-    image_0 = jnp.concatenate([mine[0].astype(F32) + got[1].astype(F32) for mine, got in products])
-    image_0 = image_0 + damp * start
-    residual = start - alpha_0 * image_0
-    values = [
-        jnp.sum(residual * residual),
-        jnp.sum(damp * residual * residual),
-        jnp.sum(damp * residual * start),
+        wait = (steps_0[3],) if k == 0 else (steps_0[-1],)
+        back.append(adjoint_call(plan, meta, near[k], far[k], (own[k], got[k]), False, wait))
+    got_back = in_turn(back, to_pair)
+
+    pairs = [
+        forward_call(plan, k, meta, near[k], far[k], False, (back[k], got_back[k])) for k in chunks
     ]
-
-    square = cross = 0.0
+    got = in_turn([send for send, _ in pairs], to_half)
+    image_0, residual, norms = zip(*[
+        residual_call(plan, k, alpha_0, damping, start, back[k], got_back[k]) for k in chunks
+    ])
+    pieces = [reduce_field(pairs[k][1], got[k]) for k in chunks]
+    scaled, stats = zip(*[
+        sensor_call(plan, k, meta, weights, pieces[k], alpha_0, damping_row, field[k])
+        for k in chunks
+    ])
+    sums, steps_1 = total(sum(norms) + jnp.pad(sum(stats), ((8, 0), (0, 0))))
+    norm_1 = sums[0]
+    beta = norm_1 / norm_0
+    curve_1 = sums[1] + 2.0 * beta * sums[2] + beta * beta * curve_0
+    alpha_1 = norm_1 / curve_1
+
+    own = [gather_field(scaled[k]) for k in chunks]
+    got = in_turn(own, to_half)
     final = []
     for k in chunks:
-        send, keep = forward_call(plan, k, meta, near[k], far[k], False, products[k])
-        factor = 1.0 - alpha_0 * piece_of(k, damping_row)
-        new_field = factor * field[k] - alpha_0 * reduce_field(send, keep)
-        new_scaled = piece_of(k, weights) * new_field
-        square = square + jnp.sum(new_scaled * new_field)
-        cross = cross + jnp.sum(new_scaled * field[k])
-        other, own = adjoint_call(plan, meta, near[k], far[k], gather_field(new_scaled), True)
-        final.append(own + to_pair(other).astype(F32))
-    sums = total(values + [square, cross])
-    norm_1 = sums[0]
-    beta = norm_1 / norm_0
-    curve_1 = (sums[1] + sums[3]) + 2.0 * beta * (sums[2] + sums[4]) + beta * beta * curve_0
-    alpha_1 = norm_1 / curve_1
-
-    image_1 = jnp.concatenate(final) + damp * residual + beta * image_0
+        wait = (steps_1[3],) if k == 0 else (steps_1[-1],)
+        sent, mine = adjoint_call(plan, meta, near[k], far[k], (own[k], got[k]), True, wait)
+        final.append(mine + to_pair(sent).astype(F32))
+    residual, image_0 = jnp.concatenate(residual), jnp.concatenate(image_0)
+    image_1 = jnp.concatenate(final) + damping[:, None, None] * residual + beta * image_0
     solution = alpha_0 * start + alpha_1 * (residual + beta * start)
     residual = residual - alpha_1 * image_1
     return solution.reshape(right_side.shape), residual.reshape(right_side.shape)

time: 268 us -> 265 us (0.989)
  waiting for transfers between devices: 61.4 us -> 102 us
  starting transfers between devices: 93.2 us -> 71.4 us
  other arithmetic: 22.3 us -> 6.19 us
  Pallas kernels: 49.2 us -> 44.9 us
    ppermute x41, waiting for transfers between devices: 50 us -> 78.8 us  [to_src(): return lax.ppermute(array, 'src', [(j, j ^ step) for j in range(n_src)])]
    ppermute x41, starting transfers between devices: 81.6 us -> 58.8 us  [to_src(): return lax.ppermute(array, 'src', [(j, j ^ step) for j in range(n_src)])]
    ppermute x9, waiting for transfers between devices: 10.3 us -> 21.9 us  [to_pair(): return lax.ppermute(array, 'sens', [(i, i ^ 2) for i in range(n_sens)])]
    reduce_sum x6 -> x4, other arithmetic: 7.97 us -> 0.47 us  [total(): return (jnp.sum(steps[-1].reshape(-1, 8 * 128), axis=1), steps)]
    pallas_call x0 -> x14, Pallas kernels: none -> 6.4 us  [the longest x4 3.61 us: sensor_call(): pl.pallas_call(kernel, in_specs=[scalars] + ([scalars] * 2 + [whole] if s...]
    pallas_call x4, Pallas kernels: 18.2 us -> 13.4 us  [adjoint_call(): pl.pallas_call(kernel, grid_spec=pltpu.PrefetchScalarGridSpec(num_scalar_...]
    pallas_call x4, Pallas kernels: 20.5 us -> 16 us  [forward_call(): pl.pallas_call(kernel, grid_spec=pltpu.PrefetchScalarGridSpec(num_scalar_...]
    unnamed x60 -> x80, local copies, waits for them, and re-layouts: 13.3 us -> 16.7 us
  transfers between devices with their start and end apart: 55 -> 55, of which waited for: 24 -> 24; matrix products, arithmetic and copies ran while one was open for 8% -> 1% of each run, Pallas kernels for 18% -> 16%
where the time goes in v2:
time: 265 us; the launch traced here: 264 us
  waiting for transfers between devices  102 us (38%)
  starting transfers between devices  71.4 us (27%)
  Pallas kernels  44.9 us (17%)
  local copies, waits for them, and re-layouts  27 us (10%)
  between operations  12.6 us (5%)
  other arithmetic  6.19 us (2%)
    ppermute x41, waiting for transfers between devices, to_src(): return lax.ppermute(array, 'src', [(j, j ^ step) for j in range(n_src)])  78.8 us
    ppermute x41, starting transfers between devices, to_src(): return lax.ppermute(array, 'src', [(j, j ^ step) for j in range(n_src)])  58.8 us
    ppermute x9, waiting for transfers between devices, to_pair(): return lax.ppermute(array, 'sens', [(i, i ^ 2) for i in range(n_sens)])  21.9 us
    unnamed x80, local copies, waits for them, and re-layouts  16.7 us
    pallas_call x4, Pallas kernels, forward_call(): pl.pallas_call(kernel, grid_spec=pltpu.PrefetchScalarGridSpec(num_scalar_...  16 us
    pallas_call x4, Pallas kernels, adjoint_call(): pl.pallas_call(kernel, grid_spec=pltpu.PrefetchScalarGridSpec(num_scalar_...  13.4 us
    ppermute x9, starting transfers between devices, to_pair(): return lax.ppermute(array, 'sens', [(i, i ^ 2) for i in range(n_sens)])  12 us
    reshape x2, local copies, waits for them, and re-layouts, half_of(): return cut.reshape(plan.pairs, part, 2, plan.sensors, plan.sources)  7.61 us
  transfers between devices with their start and end apart: 55, of which 24 were waited for; matrix products, arithmetic and copies ran while one was open for 1% of the time, Pallas kernels for 16%

profile of v2, /device:TPU:0, one launch (start us, length us, event | category | flops | bytes accessed | tf_op | source)
XLA Modules:
  0.0 264.0 jit_solution(12597483143166823757)
XLA Ops:
  6.3 2.8 %dynamic-slice_bitcast_fusion.2 = (bf16[2,16,2,128,128]{4,3,2,1,0:T(8,128)(2,1)S(1)}, bf16[2,16,2,128,128]{4,3,2,1,0:T(8,128)(2,1)S(1)}) fusion(bf16[2,2,32,2,128,128]{5,4,3,2,1,0:T(8,128)(2,1)} %bitcast.79, s32[]{:T(128)S(6)} %select_n.117, s32[]{:T(128)S(6)} %select_n.116), kind=kLoop, calls=%fused_computation.2 | loop fusion | bytes 8388616 | tf_op jit(solution)/shard_map/reshape | solution.py:424
  9.7 2.6 collective-permute-start.5
  12.2 6.9 %collective-permute-done.5.two_ref = bf16[16,64,128]{2,1,0:T(8,128)(2,1)S(1)} collective-permute-done((bf16[16,64,128]{2,1,0:T(8,128)(2,1)S(1)}, bf16[16,64,128]{2,1,0:T(8,128)(2,1)S(1)}, u32[]{:S(2)}, u32[]{:S(2)}) %collective-permute-start.5) | collective-permute-done | bytes 262176 | tf_op jit(solution)/shard_map/ppermute | solution.py:392
  19.1 2.4 forward.4
  27.0 4.8 %dynamic-slice_bitcast_fusion = (bf16[2,16,2,128,128]{4,3,2,1,0:T(8,128)(2,1)}, bf16[2,16,2,128,128]{4,3,2,1,0:T(8,128)(2,1)}) fusion(bf16[2,2,32,2,128,128]{5,4,3,2,1,0:T(8,128)(2,1)} %bitcast.80, s32[]{:T(128)S(6)} %select_n.119, s32[]{:T(128)S(6)} %select_n.118), kind=kLoop, calls=%fused_computation | loop fusion | bytes 8388616 | tf_op jit(solution)/shard_map/reshape | solution.py:424
  31.8 1.8 collective-permute-start
  35.4 1.8 collective-permute-start.1
  39.2 2.9 %collective-permute-start.2 = (f32[64,128]{1,0:T(8,128)S(1)}, f32[64,128]{1,0:T(8,128)S(1)}, u32[]{:S(2)}, u32[]{:S(2)}) collective-permute-start(f32[64,128]{1,0:T(8,128)S(1)} %pad_maximum_fusion.2), channel_id=1, source_target_pairs={{0,4},{1,5},{2,6},{3,7},{4,0},{5,1},{6,2},{7,3},{8,12},{9,13},{10,... | collective-permute-start | bytes 98312 | tf_op jit(solution)/shard_map/ppermute | solution.py:395
  42.1 2.6 collective-permute-done.11.two_ref
  46.3 5.0 %forward.5 = (bf16[16,64,256]{2,1,0:T(8,128)(2,1)}, bf16[16,64,256]{2,1,0:T(8,128)(2,1)S(1)}) custom-call(s32[4]{0:T(128)S(1)} %pad_add_fusion.2.m, bf16[2,16,2,128,128]{4,3,2,1,0:T(8,128)(2,1)S(1)} %copy-done, bf16[2,16,2,128,128]{4,3,2,1,0:T(8,128)(2,1)} %collective-permute-done.10.far_ref, f32[32,64,128]{2,1,0:T(8,128)S(1)} %bitcast.58, ...), custom_call_target="tpu_custom_call" | custom-call | flops 536870912 | bytes 4194304 | tf_op jit(solution)/shard_map/forward/pallas_call | solution.py:118
  53.1 1.9 split.4
  55.4 2.6 collective-permute-start.8
  59.3 4.6 %collective-permute-done.7.refs_2_ = bf16[256,256]{1,0:T(8,128)(2,1)} collective-permute-done((bf16[256,256]{1,0:T(8,128)(2,1)}, bf16[256,256]{1,0:T(8,128)(2,1)}, u32[]{:S(2)}, u32[]{:S(2)}) %collective-permute-start.7) | collective-permute-done | bytes 131104 | tf_op jit(solution)/shard_map/ppermute | solution.py:395
  63.9 4.9 %collective-permute-done.9.refs_4_ = bf16[256,256]{1,0:T(8,128)(2,1)} collective-permute-done((bf16[256,256]{1,0:T(8,128)(2,1)}, bf16[256,256]{1,0:T(8,128)(2,1)}, u32[]{:S(2)}, u32[]{:S(2)}) %collective-permute-start.9) | collective-permute-done | bytes 131104 | tf_op jit(solution)/shard_map/ppermute | solution.py:395
  70.7 2.5 collective-permute-start.21
  73.2 1.9 collective-permute-start.22
  79.5 2.4 collective-permute-start.14
  83.3 3.3 %collective-permute-done.23.refs_3_ = bf16[256,256]{1,0:T(8,128)(2,1)S(1)} collective-permute-done((bf16[256,256]{1,0:T(8,128)(2,1)S(1)}, bf16[256,256]{1,0:T(8,128)(2,1)S(1)}, u32[]{:S(2)}, u32[]{:S(2)}) %collective-permute-start.23) | collective-permute-done | bytes 131104 | tf_op jit(solution)/shard_map/ppermute | solution.py:395
  88.5 8.2 %collective-permute-done.14.refs_3_ = bf16[256,256]{1,0:T(8,128)(2,1)S(1)} collective-permute-done((bf16[256,256]{1,0:T(8,128)(2,1)S(1)}, bf16[256,256]{1,0:T(8,128)(2,1)S(1)}, u32[]{:S(2)}, u32[]{:S(2)}) %collective-permute-start.14) | collective-permute-done | bytes 131104 | tf_op jit(solution)/shard_map/ppermute | solution.py:395
  97.3 2.7 %collective-permute-start.26 = (bf16[256,256]{1,0:T(8,128)(2,1)S(1)}, bf16[256,256]{1,0:T(8,128)(2,1)S(1)}, u32[]{:S(2)}, u32[]{:S(2)}) collective-permute-start(bf16[256,256]{1,0:T(8,128)(2,1)S(1)} %get-tuple-element.62.refs_0_), channel_id=1, source_target_pairs={{0,2},{1,3},{2,0},{3,1},{4,6},{5,7},{6,4},{7,5},{8,10},{9,11},{10,... | collective-permute-start | bytes 393224 | tf_op jit(solution)/shard_map/ppermute | solution.py:395
  100.0 1.8 collective-permute-start.27
  103.6 3.3 %collective-permute-done.16 = f32[16,128]{1,0:T(8,128)S(1)} collective-permute-done((f32[16,128]{1,0:T(8,128)S(1)}, f32[16,128]{1,0:T(8,128)S(1)}, u32[]{:S(2)}, u32[]{:S(2)}) %collective-permute-start.16) | collective-permute-done | bytes 8224 | tf_op jit(solution)/shard_map/ppermute | solution.py:395
  107.5 4.3 %collective-permute-done.17 = f32[16,128]{1,0:T(8,128)S(1)} collective-permute-done((f32[16,128]{1,0:T(8,128)S(1)}, f32[16,128]{1,0:T(8,128)S(1)}, u32[]{:S(2)}, u32[]{:S(2)}) %collective-permute-start.17) | collective-permute-done | bytes 8224 | tf_op jit(solution)/shard_map/ppermute | solution.py:395
  113.1 3.3 %collective-permute-done.18 = f32[16,128]{1,0:T(8,128)S(1)} collective-permute-done((f32[16,128]{1,0:T(8,128)S(1)}, f32[16,128]{1,0:T(8,128)S(1)}, u32[]{:S(2)}, u32[]{:S(2)}) %collective-permute-start.18) | collective-permute-done | bytes 8224 | tf_op jit(solution)/shard_map/ppermute | solution.py:395
  116.3 1.9 adjoint.4.mine_ref.one_ref
  121.3 7.8 %collective-permute-done.19 = f32[16,128]{1,0:T(8,128)S(1)} collective-permute-done((f32[16,128]{1,0:T(8,128)S(1)}, f32[16,128]{1,0:T(8,128)S(1)}, u32[]{:S(2)}, u32[]{:S(2)}) %collective-permute-start.19) | collective-permute-done | bytes 8224 | tf_op jit(solution)/shard_map/ppermute | solution.py:392
  130.4 3.4 %forward.6 = (bf16[16,64,256]{2,1,0:T(8,128)(2,1)}, bf16[16,64,256]{2,1,0:T(8,128)(2,1)S(1)}) custom-call(s32[4]{0:T(128)S(1)} %pad_add_fusion.2.m, bf16[2,16,2,128,128]{4,3,2,1,0:T(8,128)(2,1)S(1)} %get-tuple-element.97.near_ref, bf16[2,16,2,128,128]{4,3,2,1,0:T(8,128)(2,1)S(1)} %copy-done.6, bf16[2,16,64,128]{3,2,1,0:T(8,128)(2,1)S(1)} %adjoint.4.mine_ref.one_ref, ...), custom_call_target="tpu_custom_call" | custom-call | flops 536870912 | bytes 4194304 | tf_op jit(solution)/shard_map/forward/pallas_call | solution.py:118
  134.1 4.6 %adjoint.5.refs_0_ = bf16[2,16,64,128]{3,2,1,0:T(8,128)(2,1)} custom-call(s32[4]{0:T(128)S(1)} %pad_add_fusion.2.m, bf16[2,16,2,128,128]{4,3,2,1,0:T(8,128)(2,1)S(1)} %copy-done.1, bf16[2,16,2,128,128]{4,3,2,1,0:T(8,128)(2,1)} %collective-permute-done.10.far_ref, bf16[16,64,256]{2,1,0:T(8,128)(2,1)S(1)} %ordered.10.own_ref, ...), custom_call_target="tpu_custom_call" | custom-call | flops 536870912 | bytes 4194304 | tf_op jit(solution)/shard_map/adjoint/pallas_call | solution.py:173
  140.8 7.3 %collective-permute-done.32.refs_1_ = bf16[16,64,256]{2,1,0:T(8,128)(2,1)} collective-permute-done((bf16[16,64,256]{2,1,0:T(8,128)(2,1)}, bf16[16,64,256]{2,1,0:T(8,128)(2,1)}, u32[]{:S(2)}, u32[]{:S(2)}) %collective-permute-start.32) | collective-permute-done | bytes 524320 | tf_op jit(solution)/shard_map/ppermute | solution.py:395
  149.1 1.8 split.6
  152.0 3.1 %collective-permute-start.34 = (bf16[256,256]{1,0:T(8,128)(2,1)}, bf16[256,256]{1,0:T(8,128)(2,1)}, u32[]{:S(2)}, u32[]{:S(2)}) collective-permute-start(bf16[256,256]{1,0:T(8,128)(2,1)} %get-tuple-element.69), channel_id=1, source_target_pairs={{0,4},{1,5},{2,6},{3,7},{4,0},{5,1},{6,2},{7,3},{8,12},{9,13},{10,... | collective-permute-start | bytes 393224 | tf_op jit(solution)/shard_map/ppermute | solution.py:395
  157.7 5.2 %forward.7 = (bf16[16,64,256]{2,1,0:T(8,128)(2,1)}, bf16[16,64,256]{2,1,0:T(8,128)(2,1)S(1)}) custom-call(s32[4]{0:T(128)S(1)} %pad_add_fusion.2.m, bf16[2,16,2,128,128]{4,3,2,1,0:T(8,128)(2,1)S(1)} %copy-done.2, bf16[2,16,2,128,128]{4,3,2,1,0:T(8,128)(2,1)} %collective-permute-done.10.far_ref, bf16[2,16,64,128]{3,2,1,0:T(8,128)(2,1)} %ordered.11.mine_ref.one_ref, ...), custom_call_target="tpu_custom_call" | custom-call | flops 536870912 | bytes 4194304 | tf_op jit(solution)/shard_map/forward/pallas_call | solution.py:118
  170.2 2.6 collective-permute-start.46
  174.6 7.0 %collective-permute-done.46.refs_2_ = bf16[256,256]{1,0:T(8,128)(2,1)S(1)} collective-permute-done((bf16[256,256]{1,0:T(8,128)(2,1)S(1)}, bf16[256,256]{1,0:T(8,128)(2,1)S(1)}, u32[]{:S(2)}, u32[]{:S(2)}) %collective-permute-start.46) | collective-permute-done | bytes 131104 | tf_op jit(solution)/shard_map/ppermute | solution.py:395
  185.0 2.0 collective-permute-start.37
  190.9 6.9 %collective-permute-done.38.refs_6_ = bf16[256,256]{1,0:T(8,128)(2,1)S(1)} collective-permute-done((bf16[256,256]{1,0:T(8,128)(2,1)S(1)}, bf16[256,256]{1,0:T(8,128)(2,1)S(1)}, u32[]{:S(2)}, u32[]{:S(2)}) %collective-permute-start.38) | collective-permute-done | bytes 131104 | tf_op jit(solution)/shard_map/ppermute | solution.py:395
  198.5 2.4 collective-permute-start.50
  201.5 1.8 collective-permute-start.52
  207.2 5.0 %collective-permute-done.51.refs_2_ = bf16[256,256]{1,0:T(8,128)(2,1)S(1)} collective-permute-done((bf16[256,256]{1,0:T(8,128)(2,1)S(1)}, bf16[256,256]{1,0:T(8,128)(2,1)S(1)}, u32[]{:S(2)}, u32[]{:S(2)}) %collective-permute-start.51) | collective-permute-done | bytes 131104 | tf_op jit(solution)/shard_map/ppermute | solution.py:395
  215.6 11.2 %collective-permute-done.40 = f32[24,128]{1,0:T(8,128)S(1)} collective-permute-done((f32[24,128]{1,0:T(8,128)S(1)}, f32[24,128]{1,0:T(8,128)S(1)}, u32[]{:S(2)}, u32[]{:S(2)}) %collective-permute-start.40) | collective-permute-done | bytes 12320 | tf_op jit(solution)/shard_map/ppermute | solution.py:395
  226.8 3.4 %collective-permute-start.41 = (f32[24,128]{1,0:T(8,128)S(1)}, f32[24,128]{1,0:T(8,128)S(1)}, u32[]{:S(2)}, u32[]{:S(2)}) collective-permute-start(f32[24,128]{1,0:T(8,128)S(1)} %add.143), channel_id=1, source_target_pairs={{0,2},{1,3},{2,0},{3,1},{4,6},{5,7},{6,4},{7,5},{8,10},{9,11},{10,... | collective-permute-start | bytes 36872 | tf_op jit(solution)/shard_map/ppermute | solution.py:395
  230.1 1.7 collective-permute-done.41
  232.8 3.6 %collective-permute-done.42 = f32[24,128]{1,0:T(8,128)S(1)} collective-permute-done((f32[24,128]{1,0:T(8,128)S(1)}, f32[24,128]{1,0:T(8,128)S(1)}, u32[]{:S(2)}, u32[]{:S(2)}) %collective-permute-start.42) | collective-permute-done | bytes 12320 | tf_op jit(solution)/shard_map/ppermute | solution.py:395
  237.9 2.2 collective-permute-done.43
  240.1 1.9 adjoint.6
  246.2 5.0 %adjoint.7 = (bf16[16,64,128]{2,1,0:T(8,128)(2,1)}, f32[16,64,128]{2,1,0:T(8,128)S(1)}) custom-call(s32[4]{0:T(128)S(1)} %pad_add_fusion.2.m, bf16[2,16,2,128,128]{4,3,2,1,0:T(8,128)(2,1)S(1)} %copy-done.3, bf16[2,16,2,128,128]{4,3,2,1,0:T(8,128)(2,1)} %collective-permute-done.10.far_ref, bf16[16,64,256]{2,1,0:T(8,128)(2,1)} %ordered.13.own_ref, ...), custom_call_target="tpu_custom_call" | custom-call | flops 536870912 | bytes 4194304 | tf_op jit(solution)/shard_map/adjoint/pallas_call | solution.py:173
  258.5 2.4 collective-permute-done.54
  262.1 1.9 fusion.2
  (211 shorter events, 74.1 us)
Async XLA Ops:
  9.2 10.0 %collective-permute-start.4 = (bf16[2,16,2,128,128]{4,3,2,1,0:T(8,128)(2,1)S(1)}, bf16[2,16,2,128,128]{4,3,2,1,0:T(8,128)(2,1)S(1)}, u32[]{:S(2)}, u32[]{:S(2)}) collective-permute-start(bf16[2,16,2,128,128]{4,3,2,1,0:T(8,128)(2,1)S(1)} %get-tuple-element.96), channel_id=1, source_target_pairs={{0,8},{8,0},{16,24},{24,16},{1,9},{9,1},{17,25},{25,17},{2,10},{10... | collective-permute-start | bytes 6291464 | tf_op jit(solution)/shard_map/ppermute | solution.py:389
  9.7 9.5 %collective-permute-start.5 = (bf16[16,64,128]{2,1,0:T(8,128)(2,1)S(1)}, bf16[16,64,128]{2,1,0:T(8,128)(2,1)S(1)}, u32[]{:S(2)}, u32[]{:S(2)}) collective-permute-start(bf16[16,64,128]{2,1,0:T(8,128)(2,1)S(1)} %bitcast.70), channel_id=1, source_target_pairs={{0,16},{8,24},{16,0},{24,8},{1,17},{9,25},{17,1},{25,9},{2,18},{10... | collective-permute-start | bytes 786440 | tf_op jit(solution)/shard_map/ppermute | solution.py:392
  31.8 12.9 %collective-permute-start.10 = (bf16[2,16,2,128,128]{4,3,2,1,0:T(8,128)(2,1)}, bf16[2,16,2,128,128]{4,3,2,1,0:T(8,128)(2,1)}, u32[]{:S(2)}, u32[]{:S(2)}) collective-permute-start(bf16[2,16,2,128,128]{4,3,2,1,0:T(8,128)(2,1)} %get-tuple-element.94), channel_id=1, source_target_pairs={{0,8},{8,0},{16,24},{24,16},{1,9},{9,1},{17,25},{25,17},{2,10},{10... | collective-permute-start | bytes 6291464 | tf_op jit(solution)/shard_map/ppermute | solution.py:389
  33.6 17.8 %collective-permute-start.6 = (bf16[16,64,256]{2,1,0:T(8,128)(2,1)}, bf16[16,64,256]{2,1,0:T(8,128)(2,1)}, u32[]{:S(2)}, u32[]{:S(2)}) collective-permute-start(bf16[16,64,256]{2,1,0:T(8,128)(2,1)} %copy-done.22), channel_id=1, source_target_pairs={{0,1},{1,0},{2,3},{3,2},{4,5},{5,4},{6,7},{7,6},{8,9},{9,8},{10,11... | collective-permute-start | bytes 1572872 | tf_op jit(solution)/shard_map/ppermute | solution.py:395
  37.3 7.4 %collective-permute-start.11 = (bf16[16,64,128]{2,1,0:T(8,128)(2,1)S(1)}, bf16[16,64,128]{2,1,0:T(8,128)(2,1)}, u32[]{:S(2)}, u32[]{:S(2)}) collective-permute-start(bf16[16,64,128]{2,1,0:T(8,128)(2,1)S(1)} %bitcast.68), channel_id=1, source_target_pairs={{0,16},{8,24},{16,0},{24,8},{1,17},{9,25},{17,1},{25,9},{2,18},{10... | collective-permute-start | bytes 786440 | tf_op jit(solution)/shard_map/ppermute | solution.py:392
  39.2 13.7 %collective-permute-start.2 = (f32[64,128]{1,0:T(8,128)S(1)}, f32[64,128]{1,0:T(8,128)S(1)}, u32[]{:S(2)}, u32[]{:S(2)}) collective-permute-start(f32[64,128]{1,0:T(8,128)S(1)} %pad_maximum_fusion.2), channel_id=1, source_target_pairs={{0,4},{1,5},{2,6},{3,7},{4,0},{5,1},{6,2},{7,3},{8,12},{9,13},{10,... | collective-permute-start | bytes 98312 | tf_op jit(solution)/shard_map/ppermute | solution.py:395
  51.3 25.3 %collective-permute-start.12 = (bf16[16,64,256]{2,1,0:T(8,128)(2,1)}, bf16[16,64,256]{2,1,0:T(8,128)(2,1)}, u32[]{:S(2)}, u32[]{:S(2)}) collective-permute-start(bf16[16,64,256]{2,1,0:T(8,128)(2,1)} %ordered.9), channel_id=1, source_target_pairs={{0,1},{1,0},{2,3},{3,2},{4,5},{5,4},{6,7},{7,6},{8,9},{9,8},{10,11... | collective-permute-start | bytes 1572872 | tf_op jit(solution)/shard_map/ppermute | solution.py:395
  53.0 6.3 %collective-permute-start.3 = (f32[2,32,128]{2,1,0:T(8,128)S(1)}, f32[2,32,128]{2,1,0:T(8,128)S(1)}, u32[]{:S(2)}, u32[]{:S(2)}) collective-permute-start(f32[2,32,128]{2,1,0:T(8,128)S(1)} %get-tuple-element.102), channel_id=1, source_target_pairs={{0,8},{8,0},{16,24},{24,16},{1,9},{9,1},{17,25},{25,17},{2,10},{10... | collective-permute-start | bytes 98312 | tf_op jit(solution)/shard_map/ppermute | solution.py:389
  54.9 9.0 %collective-permute-start.7 = (bf16[256,256]{1,0:T(8,128)(2,1)}, bf16[256,256]{1,0:T(8,128)(2,1)}, u32[]{:S(2)}, u32[]{:S(2)}) collective-permute-start(bf16[256,256]{1,0:T(8,128)(2,1)} %get-tuple-element.49), channel_id=1, source_target_pairs={{0,2},{1,3},{2,0},{3,1},{4,6},{5,7},{6,4},{7,5},{8,10},{9,11},{10,... | collective-permute-start | bytes 393224 | tf_op jit(solution)/shard_map/ppermute | solution.py:395
  55.4 8.6 %collective-permute-start.8 = (bf16[256,256]{1,0:T(8,128)(2,1)}, bf16[256,256]{1,0:T(8,128)(2,1)}, u32[]{:S(2)}, u32[]{:S(2)}) collective-permute-start(bf16[256,256]{1,0:T(8,128)(2,1)} %get-tuple-element.50), channel_id=1, source_target_pairs={{0,4},{1,5},{2,6},{3,7},{4,0},{5,1},{6,2},{7,3},{8,12},{9,13},{10,... | collective-permute-start | bytes 393224 | tf_op jit(solution)/shard_map/ppermute | solution.py:395
  58.0 10.9 %collective-permute-start.9 = (bf16[256,256]{1,0:T(8,128)(2,1)}, bf16[256,256]{1,0:T(8,128)(2,1)}, u32[]{:S(2)}, u32[]{:S(2)}) collective-permute-start(bf16[256,256]{1,0:T(8,128)(2,1)} %get-tuple-element.51), channel_id=1, source_target_pairs={{0,6},{1,7},{2,4},{3,5},{4,2},{5,3},{6,0},{7,1},{8,14},{9,15},{10,... | collective-permute-start | bytes 393224 | tf_op jit(solution)/shard_map/ppermute | solution.py:395
  70.7 11.1 %collective-permute-start.21 = (bf16[256,256]{1,0:T(8,128)(2,1)S(1)}, bf16[256,256]{1,0:T(8,128)(2,1)S(1)}, u32[]{:S(2)}, u32[]{:S(2)}) collective-permute-start(bf16[256,256]{1,0:T(8,128)(2,1)S(1)} %get-tuple-element.60.refs_0_), channel_id=1, source_target_pairs={{0,2},{1,3},{2,0},{3,1},{4,6},{5,7},{6,4},{7,5},{8,10},{9,11},{10,... | collective-permute-start | bytes 393224 | tf_op jit(solution)/shard_map/ppermute | solution.py:395
  73.2 10.1 %collective-permute-start.22 = (bf16[256,256]{1,0:T(8,128)(2,1)S(1)}, bf16[256,256]{1,0:T(8,128)(2,1)S(1)}, u32[]{:S(2)}, u32[]{:S(2)}) collective-permute-start(bf16[256,256]{1,0:T(8,128)(2,1)S(1)} %get-tuple-element.60.refs_0_), channel_id=1, source_target_pairs={{0,4},{1,5},{2,6},{3,7},{4,0},{5,1},{6,2},{7,3},{8,12},{9,13},{10,... | collective-permute-start | bytes 393224 | tf_op jit(solution)/shard_map/ppermute | solution.py:395
  75.2 11.5 %collective-permute-start.23 = (bf16[256,256]{1,0:T(8,128)(2,1)S(1)}, bf16[256,256]{1,0:T(8,128)(2,1)S(1)}, u32[]{:S(2)}, u32[]{:S(2)}) collective-permute-start(bf16[256,256]{1,0:T(8,128)(2,1)S(1)} %get-tuple-element.60.refs_0_), channel_id=1, source_target_pairs={{0,6},{1,7},{2,4},{3,5},{4,2},{5,3},{6,0},{7,1},{8,14},{9,15},{10,... | collective-permute-start | bytes 393224 | tf_op jit(solution)/shard_map/ppermute | solution.py:395
  78.9 9.6 %collective-permute-start.13 = (bf16[256,256]{1,0:T(8,128)(2,1)S(1)}, bf16[256,256]{1,0:T(8,128)(2,1)S(1)}, u32[]{:S(2)}, u32[]{:S(2)}) collective-permute-start(bf16[256,256]{1,0:T(8,128)(2,1)S(1)} %get-tuple-element.56), channel_id=1, source_target_pairs={{0,2},{1,3},{2,0},{3,1},{4,6},{5,7},{6,4},{7,5},{8,10},{9,11},{10,... | collective-permute-start | bytes 393224 | tf_op jit(solution)/shard_map/ppermute | solution.py:395
  79.5 17.2 %collective-permute-start.14 = (bf16[256,256]{1,0:T(8,128)(2,1)S(1)}, bf16[256,256]{1,0:T(8,128)(2,1)S(1)}, u32[]{:S(2)}, u32[]{:S(2)}) collective-permute-start(bf16[256,256]{1,0:T(8,128)(2,1)S(1)} %get-tuple-element.57), channel_id=1, source_target_pairs={{0,4},{1,5},{2,6},{3,7},{4,0},{5,1},{6,2},{7,3},{8,12},{9,13},{10,... | collective-permute-start | bytes 393224 | tf_op jit(solution)/shard_map/ppermute | solution.py:395
  81.8 14.8 %collective-permute-start.15 = (bf16[256,256]{1,0:T(8,128)(2,1)S(1)}, bf16[256,256]{1,0:T(8,128)(2,1)S(1)}, u32[]{:S(2)}, u32[]{:S(2)}) collective-permute-start(bf16[256,256]{1,0:T(8,128)(2,1)S(1)} %get-tuple-element.58), channel_id=1, source_target_pairs={{0,6},{1,7},{2,4},{3,5},{4,2},{5,3},{6,0},{7,1},{8,14},{9,15},{10,... | collective-permute-start | bytes 393224 | tf_op jit(solution)/shard_map/ppermute | solution.py:395
  87.2 29.1 %collective-permute-start.24 = (bf16[16,64,256]{2,1,0:T(8,128)(2,1)S(1)}, bf16[16,64,256]{2,1,0:T(8,128)(2,1)S(1)}, u32[]{:S(2)}, u32[]{:S(2)}) collective-permute-start(bf16[16,64,256]{2,1,0:T(8,128)(2,1)S(1)} %bitcast.65), channel_id=1, source_target_pairs={{0,1},{1,0},{2,3},{3,2},{4,5},{5,4},{6,7},{7,6},{8,9},{9,8},{10,11... | collective-permute-start | bytes 1572872 | tf_op jit(solution)/shard_map/ppermute | solution.py:395
  97.3 22.5 %collective-permute-start.26 = (bf16[256,256]{1,0:T(8,128)(2,1)S(1)}, bf16[256,256]{1,0:T(8,128)(2,1)S(1)}, u32[]{:S(2)}, u32[]{:S(2)}) collective-permute-start(bf16[256,256]{1,0:T(8,128)(2,1)S(1)} %get-tuple-element.62.refs_0_), channel_id=1, source_target_pairs={{0,2},{1,3},{2,0},{3,1},{4,6},{5,7},{6,4},{7,5},{8,10},{9,11},{10,... | collective-permute-start | bytes 393224 | tf_op jit(solution)/shard_map/ppermute | solution.py:395
  100.0 19.8 %collective-permute-start.27 = (bf16[256,256]{1,0:T(8,128)(2,1)S(1)}, bf16[256,256]{1,0:T(8,128)(2,1)S(1)}, u32[]{:S(2)}, u32[]{:S(2)}) collective-permute-start(bf16[256,256]{1,0:T(8,128)(2,1)S(1)} %get-tuple-element.62.refs_0_), channel_id=1, source_target_pairs={{0,4},{1,5},{2,6},{3,7},{4,0},{5,1},{6,2},{7,3},{8,12},{9,13},{10,... | collective-permute-start | bytes 393224 | tf_op jit(solution)/shard_map/ppermute | solution.py:395
  101.8 18.0 %collective-permute-start.28 = (bf16[256,256]{1,0:T(8,128)(2,1)S(1)}, bf16[256,256]{1,0:T(8,128)(2,1)S(1)}, u32[]{:S(2)}, u32[]{:S(2)}) collective-permute-start(bf16[256,256]{1,0:T(8,128)(2,1)S(1)} %get-tuple-element.62.refs_0_), channel_id=1, source_target_pairs={{0,6},{1,7},{2,4},{3,5},{4,2},{5,3},{6,0},{7,1},{8,14},{9,15},{10,... | collective-permute-start | bytes 393224 | tf_op jit(solution)/shard_map/ppermute | solution.py:395
  106.9 4.9 %collective-permute-start.17 = (f32[16,128]{1,0:T(8,128)S(1)}, f32[16,128]{1,0:T(8,128)S(1)}, u32[]{:S(2)}, u32[]{:S(2)}) collective-permute-start(f32[16,128]{1,0:T(8,128)S(1)} %add.135), channel_id=1, source_target_pairs={{0,2},{1,3},{2,0},{3,1},{4,6},{5,7},{6,4},{7,5},{8,10},{9,11},{10,... | collective-permute-start | bytes 24584 | tf_op jit(solution)/shard_map/ppermute | solution.py:395
  118.2 12.1 %collective-permute-start.25 = (bf16[2,16,64,128]{3,2,1,0:T(8,128)(2,1)S(1)}, bf16[2,16,64,128]{3,2,1,0:T(8,128)(2,1)S(1)}, u32[]{:S(2)}, u32[]{:S(2)}) collective-permute-start(bf16[2,16,64,128]{3,2,1,0:T(8,128)(2,1)S(1)} %adjoint.4.mine_ref.one_ref), channel_id=1, source_target_pairs={{0,16},{8,24},{16,0},{24,8},{1,17},{9,25},{17,1},{25,9},{2,18},{10... | collective-permute-start | bytes 1572872 | tf_op jit(solution)/shard_map/ppermute | solution.py:392
  120.4 13.7 %collective-permute-start.29 = (bf16[16,64,256]{2,1,0:T(8,128)(2,1)S(1)}, bf16[16,64,256]{2,1,0:T(8,128)(2,1)S(1)}, u32[]{:S(2)}, u32[]{:S(2)}) collective-permute-start(bf16[16,64,256]{2,1,0:T(8,128)(2,1)S(1)} %ordered.10.own_ref), channel_id=1, source_target_pairs={{0,1},{1,0},{2,3},{3,2},{4,5},{5,4},{6,7},{7,6},{8,9},{9,8},{10,11... | collective-permute-start | bytes 1572872 | tf_op jit(solution)/shard_map/ppermute | solution.py:395
  120.6 8.5 %collective-permute-start.19 = (f32[16,128]{1,0:T(8,128)S(1)}, f32[16,128]{1,0:T(8,128)S(1)}, u32[]{:S(2)}, u32[]{:S(2)}) collective-permute-start(f32[16,128]{1,0:T(8,128)S(1)} %add.137.outs_0_), channel_id=1, source_target_pairs={{0,16},{8,24},{16,0},{24,8},{1,17},{9,25},{17,1},{25,9},{2,18},{10... | collective-permute-start | bytes 24584 | tf_op jit(solution)/shard_map/ppermute | solution.py:392
  133.8 14.3 %collective-permute-start.32 = (bf16[16,64,256]{2,1,0:T(8,128)(2,1)}, bf16[16,64,256]{2,1,0:T(8,128)(2,1)}, u32[]{:S(2)}, u32[]{:S(2)}) collective-permute-start(bf16[16,64,256]{2,1,0:T(8,128)(2,1)} %get-tuple-element.66), channel_id=1, source_target_pairs={{0,1},{1,0},{2,3},{3,2},{4,5},{5,4},{6,7},{7,6},{8,9},{9,8},{10,11... | collective-permute-start | bytes 1572872 | tf_op jit(solution)/shard_map/ppermute | solution.py:395
  138.7 17.4 %collective-permute-start.30 = (bf16[2,16,64,128]{3,2,1,0:T(8,128)(2,1)}, bf16[2,16,64,128]{3,2,1,0:T(8,128)(2,1)}, u32[]{:S(2)}, u32[]{:S(2)}) collective-permute-start(bf16[2,16,64,128]{3,2,1,0:T(8,128)(2,1)} %ordered.11.mine_ref.one_ref), channel_id=1, source_target_pairs={{0,16},{8,24},{16,0},{24,8},{1,17},{9,25},{17,1},{25,9},{2,18},{10... | collective-permute-start | bytes 1572872 | tf_op jit(solution)/shard_map/ppermute | solution.py:392
  140.1 23.9 %collective-permute-start.31 = (f32[32]{0:T(128)S(1)}, f32[32]{0:T(128)S(1)}, u32[]{:S(2)}, u32[]{:S(2)}) collective-permute-start(f32[32]{0:T(128)S(1)} %copy-done.37), channel_id=1, source_target_pairs={{0,16},{8,24},{16,0},{24,8},{1,17},{9,25},{17,1},{25,9},{2,18},{10... | collective-permute-start | bytes 392 | tf_op jit(solution)/shard_map/ppermute | solution.py:392
  151.7 14.5 %collective-permute-start.33 = (bf16[256,256]{1,0:T(8,128)(2,1)}, bf16[256,256]{1,0:T(8,128)(2,1)}, u32[]{:S(2)}, u32[]{:S(2)}) collective-permute-start(bf16[256,256]{1,0:T(8,128)(2,1)} %get-tuple-element.68), channel_id=1, source_target_pairs={{0,2},{1,3},{2,0},{3,1},{4,6},{5,7},{6,4},{7,5},{8,10},{9,11},{10,... | collective-permute-start | bytes 393224 | tf_op jit(solution)/shard_map/ppermute | solution.py:395
  152.0 14.3 %collective-permute-start.34 = (bf16[256,256]{1,0:T(8,128)(2,1)}, bf16[256,256]{1,0:T(8,128)(2,1)}, u32[]{:S(2)}, u32[]{:S(2)}) collective-permute-start(bf16[256,256]{1,0:T(8,128)(2,1)} %get-tuple-element.69), channel_id=1, source_target_pairs={{0,4},{1,5},{2,6},{3,7},{4,0},{5,1},{6,2},{7,3},{8,12},{9,13},{10,... | collective-permute-start | bytes 393224 | tf_op jit(solution)/shard_map/ppermute | solution.py:395
  155.0 11.2 %collective-permute-start.35 = (bf16[256,256]{1,0:T(8,128)(2,1)}, bf16[256,256]{1,0:T(8,128)(2,1)}, u32[]{:S(2)}, u32[]{:S(2)}) collective-permute-start(bf16[256,256]{1,0:T(8,128)(2,1)} %get-tuple-element.70), channel_id=1, source_target_pairs={{0,6},{1,7},{2,4},{3,5},{4,2},{5,3},{6,0},{7,1},{8,14},{9,15},{10,... | collective-permute-start | bytes 393224 | tf_op jit(solution)/shard_map/ppermute | solution.py:395
  163.6 20.2 %collective-permute-start.36 = (bf16[16,64,256]{2,1,0:T(8,128)(2,1)}, bf16[16,64,256]{2,1,0:T(8,128)(2,1)}, u32[]{:S(2)}, u32[]{:S(2)}) collective-permute-start(bf16[16,64,256]{2,1,0:T(8,128)(2,1)} %ordered.12), channel_id=1, source_target_pairs={{0,1},{1,0},{2,3},{3,2},{4,5},{5,4},{6,7},{7,6},{8,9},{9,8},{10,11... | collective-permute-start | bytes 1572872 | tf_op jit(solution)/shard_map/ppermute | solution.py:395
  169.4 5.2 %collective-permute-start.45 = (bf16[256,256]{1,0:T(8,128)(2,1)S(1)}, bf16[256,256]{1,0:T(8,128)(2,1)S(1)}, u32[]{:S(2)}, u32[]{:S(2)}) collective-permute-start(bf16[256,256]{1,0:T(8,128)(2,1)S(1)} %get-tuple-element.82.refs_0_), channel_id=1, source_target_pairs={{0,2},{1,3},{2,0},{3,1},{4,6},{5,7},{6,4},{7,5},{8,10},{9,11},{10,... | collective-permute-start | bytes 393224 | tf_op jit(solution)/shard_map/ppermute | solution.py:395
  170.2 11.4 %collective-permute-start.46 = (bf16[256,256]{1,0:T(8,128)(2,1)S(1)}, bf16[256,256]{1,0:T(8,128)(2,1)S(1)}, u32[]{:S(2)}, u32[]{:S(2)}) collective-permute-start(bf16[256,256]{1,0:T(8,128)(2,1)S(1)} %get-tuple-element.82.refs_0_), channel_id=1, source_target_pairs={{0,4},{1,5},{2,6},{3,7},{4,0},{5,1},{6,2},{7,3},{8,12},{9,13},{10,... | collective-permute-start | bytes 393224 | tf_op jit(solution)/shard_map/ppermute | solution.py:395
  172.8 8.9 %collective-permute-start.47 = (bf16[256,256]{1,0:T(8,128)(2,1)S(1)}, bf16[256,256]{1,0:T(8,128)(2,1)S(1)}, u32[]{:S(2)}, u32[]{:S(2)}) collective-permute-start(bf16[256,256]{1,0:T(8,128)(2,1)S(1)} %get-tuple-element.82.refs_0_), channel_id=1, source_target_pairs={{0,6},{1,7},{2,4},{3,5},{4,2},{5,3},{6,0},{7,1},{8,14},{9,15},{10,... | collective-permute-start | bytes 393224 | tf_op jit(solution)/shard_map/ppermute | solution.py:395
  182.3 31.3 %collective-permute-start.48 = (bf16[16,64,256]{2,1,0:T(8,128)(2,1)S(1)}, bf16[16,64,256]{2,1,0:T(8,128)(2,1)S(1)}, u32[]{:S(2)}, u32[]{:S(2)}) collective-permute-start(bf16[16,64,256]{2,1,0:T(8,128)(2,1)S(1)} %bitcast.63), channel_id=1, source_target_pairs={{0,1},{1,0},{2,3},{3,2},{4,5},{5,4},{6,7},{7,6},{8,9},{9,8},{10,11... | collective-permute-start | bytes 1572872 | tf_op jit(solution)/shard_map/ppermute | solution.py:395
  185.0 5.9 %collective-permute-start.37 = (bf16[256,256]{1,0:T(8,128)(2,1)S(1)}, bf16[256,256]{1,0:T(8,128)(2,1)S(1)}, u32[]{:S(2)}, u32[]{:S(2)}) collective-permute-start(bf16[256,256]{1,0:T(8,128)(2,1)S(1)} %get-tuple-element.76), channel_id=1, source_target_pairs={{0,2},{1,3},{2,0},{3,1},{4,6},{5,7},{6,4},{7,5},{8,10},{9,11},{10,... | collective-permute-start | bytes 393224 | tf_op jit(solution)/shard_map/ppermute | solution.py:395
  187.1 10.8 %collective-permute-start.38 = (bf16[256,256]{1,0:T(8,128)(2,1)S(1)}, bf16[256,256]{1,0:T(8,128)(2,1)S(1)}, u32[]{:S(2)}, u32[]{:S(2)}) collective-permute-start(bf16[256,256]{1,0:T(8,128)(2,1)S(1)} %get-tuple-element.77), channel_id=1, source_target_pairs={{0,4},{1,5},{2,6},{3,7},{4,0},{5,1},{6,2},{7,3},{8,12},{9,13},{10,... | collective-permute-start | bytes 393224 | tf_op jit(solution)/shard_map/ppermute | solution.py:395
  188.1 9.7 %collective-permute-start.39 = (bf16[256,256]{1,0:T(8,128)(2,1)S(1)}, bf16[256,256]{1,0:T(8,128)(2,1)S(1)}, u32[]{:S(2)}, u32[]{:S(2)}) collective-permute-start(bf16[256,256]{1,0:T(8,128)(2,1)S(1)} %get-tuple-element.78), channel_id=1, source_target_pairs={{0,6},{1,7},{2,4},{3,5},{4,2},{5,3},{6,0},{7,1},{8,14},{9,15},{10,... | collective-permute-start | bytes 393224 | tf_op jit(solution)/shard_map/ppermute | solution.py:395
  198.5 8.7 %collective-permute-start.50 = (bf16[256,256]{1,0:T(8,128)(2,1)S(1)}, bf16[256,256]{1,0:T(8,128)(2,1)S(1)}, u32[]{:S(2)}, u32[]{:S(2)}) collective-permute-start(bf16[256,256]{1,0:T(8,128)(2,1)S(1)} %get-tuple-element.85.refs_0_), channel_id=1, source_target_pairs={{0,2},{1,3},{2,0},{3,1},{4,6},{5,7},{6,4},{7,5},{8,10},{9,11},{10,... | collective-permute-start | bytes 393224 | tf_op jit(solution)/shard_map/ppermute | solution.py:395
  200.9 11.3 %collective-permute-start.51 = (bf16[256,256]{1,0:T(8,128)(2,1)S(1)}, bf16[256,256]{1,0:T(8,128)(2,1)S(1)}, u32[]{:S(2)}, u32[]{:S(2)}) collective-permute-start(bf16[256,256]{1,0:T(8,128)(2,1)S(1)} %get-tuple-element.85.refs_0_), channel_id=1, source_target_pairs={{0,4},{1,5},{2,6},{3,7},{4,0},{5,1},{6,2},{7,3},{8,12},{9,13},{10,... | collective-permute-start | bytes 393224 | tf_op jit(solution)/shard_map/ppermute | solution.py:395
  201.5 10.7 %collective-permute-start.52 = (bf16[256,256]{1,0:T(8,128)(2,1)S(1)}, bf16[256,256]{1,0:T(8,128)(2,1)S(1)}, u32[]{:S(2)}, u32[]{:S(2)}) collective-permute-start(bf16[256,256]{1,0:T(8,128)(2,1)S(1)} %get-tuple-element.85.refs_0_), channel_id=1, source_target_pairs={{0,6},{1,7},{2,4},{3,5},{4,2},{5,3},{6,0},{7,1},{8,14},{9,15},{10,... | collective-permute-start | bytes 393224 | tf_op jit(solution)/shard_map/ppermute | solution.py:395
  213.6 31.1 %collective-permute-start.53 = (bf16[16,64,256]{2,1,0:T(8,128)(2,1)}, bf16[16,64,256]{2,1,0:T(8,128)(2,1)}, u32[]{:S(2)}, u32[]{:S(2)}) collective-permute-start(bf16[16,64,256]{2,1,0:T(8,128)(2,1)} %ordered.13.own_ref), channel_id=1, source_target_pairs={{0,1},{1,0},{2,3},{3,2},{4,5},{5,4},{6,7},{7,6},{8,9},{9,8},{10,11... | collective-permute-start | bytes 1572872 | tf_op jit(solution)/shard_map/ppermute | solution.py:395
  214.4 12.3 %collective-permute-start.40 = (f32[24,128]{1,0:T(8,128)S(1)}, f32[24,128]{1,0:T(8,128)S(1)}, u32[]{:S(2)}, u32[]{:S(2)}) collective-permute-start(f32[24,128]{1,0:T(8,128)S(1)} %pad_add_fusion), channel_id=1, source_target_pairs={{0,1},{1,0},{2,3},{3,2},{4,5},{5,4},{6,7},{7,6},{8,9},{9,8},{10,11... | collective-permute-start | bytes 36872 | tf_op jit(solution)/shard_map/ppermute | solution.py:395
  226.8 5.0 %collective-permute-start.41 = (f32[24,128]{1,0:T(8,128)S(1)}, f32[24,128]{1,0:T(8,128)S(1)}, u32[]{:S(2)}, u32[]{:S(2)}) collective-permute-start(f32[24,128]{1,0:T(8,128)S(1)} %add.143), channel_id=1, source_target_pairs={{0,2},{1,3},{2,0},{3,1},{4,6},{5,7},{6,4},{7,5},{8,10},{9,11},{10,... | collective-permute-start | bytes 36872 | tf_op jit(solution)/shard_map/ppermute | solution.py:395
  231.8 4.6 %collective-permute-start.42 = (f32[24,128]{1,0:T(8,128)S(1)}, f32[24,128]{1,0:T(8,128)S(1)}, u32[]{:S(2)}, u32[]{:S(2)}) collective-permute-start(f32[24,128]{1,0:T(8,128)S(1)} %add.144), channel_id=1, source_target_pairs={{0,4},{1,5},{2,6},{3,7},{4,0},{5,1},{6,2},{7,3},{8,12},{9,13},{10,... | collective-permute-start | bytes 36872 | tf_op jit(solution)/shard_map/ppermute | solution.py:395
  242.8 14.5 %collective-permute-start.49 = (bf16[16,64,128]{2,1,0:T(8,128)(2,1)S(1)}, bf16[16,64,128]{2,1,0:T(8,128)(2,1)}, u32[]{:S(2)}, u32[]{:S(2)}) collective-permute-start(bf16[16,64,128]{2,1,0:T(8,128)(2,1)S(1)} %get-tuple-element.84), channel_id=1, source_target_pairs={{0,16},{8,24},{16,0},{24,8},{1,17},{9,25},{17,1},{25,9},{2,18},{10... | collective-permute-start | bytes 786440 | tf_op jit(solution)/shard_map/ppermute | solution.py:392
  252.1 8.8 %collective-permute-start.54 = (bf16[16,64,128]{2,1,0:T(8,128)(2,1)}, bf16[16,64,128]{2,1,0:T(8,128)(2,1)}, u32[]{:S(2)}, u32[]{:S(2)}) collective-permute-start(bf16[16,64,128]{2,1,0:T(8,128)(2,1)} %get-tuple-element.87), channel_id=1, source_target_pairs={{0,16},{8,24},{16,0},{24,8},{1,17},{9,25},{17,1},{25,9},{2,18},{10... | collective-permute-start | bytes 786440 | tf_op jit(solution)/shard_map/ppermute | solution.py:392
  (46 other events, 419.3 us)
